TPU v7x, 256 devices: a whole 4x4x8 slice. The times are simulated.
256 devices in a mesh: gx: 32 (over z, x), gy: 8 (over y, core).
Axes of the slice: x: 4, y: 4, z: 8, core: 2. Of those that a mesh axis runs over, the one named last changes fastest.
Arguments:
- pressure: float32 [10, 256, 1024], P(None, 'gx', 'gy'), may hold values from -3 to 1
- saturation_old: float32 [10, 256, 1024], P(None, 'gx', 'gy'), may hold values from 0.3 to 1
- soil_type: int32 [10, 256, 1024], P(None, 'gx', 'gy'), may hold values from 0 to 23
- recharge: float32 [256, 1024], P('gx', 'gy'), may hold values from -6 to 6
- ksat_table: float32 [24], replicated, may hold values from 0.05 to 5
- alpha_table: float32 [24], replicated, may hold values from 0.3 to 3
- porosity_table: float32 [24], replicated, may hold values from 0.1 to 0.5
- residual_table: float32 [24], replicated, may hold values from 0.02 to 0.3
Outputs:
- pressure_new: float32 [10, 256, 1024], P(None, 'gx', 'gy')
All inputs are finite; a program needn't handle non-finite values.
Results may differ from a plain program's by a relative error of at most 0.0003.
Values sent between devices are 32-bit elements; how exact they have to be, the bound alone decides.
No kernel may reach another device: no remote copies, remote signals or barrier semaphores. Data moves between devices by JAX's collectives and lax.ppermute only.
A program may use at most 64 MiB of HBM per device.

v0:
```python
import functools

import jax
import jax.numpy as jnp
from jax import lax
from jax.experimental import pallas as pl
from jax.experimental.pallas import tpu as pltpu
from jax.sharding import PartitionSpec as P


NZ = 10
BX = 8
BY = 128
REACH = 4
ROWS = (2 * REACH + 1) * BX
SA = 24
SB = 16
LANES = 128
OWN_S = REACH * BX // 4
OMEGA = 0.8
STORAGE = 0.05
EPSILON = 1e-06
F32 = jnp.float32


def lane_roll(v, shift):
    return pltpu.roll(v, shift % v.shape[1], 1)


def row_roll(v, shift):
    return pltpu.roll(v, shift % v.shape[0], 0)


def lanes_of(rows, width=LANES):
    return lax.broadcasted_iota(jnp.int32, (rows, width), 1)


def rows_of(rows, width=LANES):
    return lax.broadcasted_iota(jnp.int32, (rows, width), 0)


def pair_sum(u, step):
    low = (lanes_of(u.shape[0]) & step) == 0
    return u + jnp.where(low, lane_roll(u, -step), lane_roll(u, step))


def from_south(u, step):
    low = (lanes_of(u.shape[0]) & step) == 0
    return jnp.where(low, u, lane_roll(u, step))


def each_layer(body, together, count=NZ):
    if together == count:
        for k in range(count):
            body(k)
        return

    def step(i, carry):
        for j in range(together):
            body(together * i + j)
        return carry

    lax.fori_loop(0, count // together, step, 0)


def below(k):
    return max(k - 1, 0) if isinstance(k, int) else jnp.maximum(k - 1, 0)


def above(k):
    return min(k + 1, NZ - 1) if isinstance(k, int) else jnp.minimum(k + 1, NZ - 1)


def one_if(condition):
    return jnp.where(condition, 1.0, 0.0).astype(F32)


class Level:
    def __init__(self, storage, west, south, lower, gain, across, along, rows):
        self.storage, self.west, self.south, self.lower, self.gain = storage, west, south, lower, gain
        self.across, self.along, self.rows = across, along, rows
        self.parts = across * along

    def load(self, src, k):
        return [src[k, j, 0 : self.rows, :] for j in range(self.parts)]

    def from_west(self, v):
        n = self.along
        return [v[j - n] if j >= n else row_roll(v[self.parts - n + j], 1) for j in range(self.parts)]

    def from_east(self, v):
        n, m = self.along, self.parts
        return [v[j + n] if j + n < m else row_roll(v[j + n - m], -1) for j in range(m)]

    def from_south(self, v):
        n = self.along
        return [v[j - 1] if j % n else lane_roll(v[j + n - 1], 1) for j in range(self.parts)]

    def from_north(self, v):
        n = self.along
        return [v[j + 1] if (j + 1) % n else lane_roll(v[j + 1 - n], -1) for j in range(self.parts)]

    def diagonals(self, k):
        west, south = self.load(self.west, k), self.load(self.south, k)
        east, north = self.from_east(west), self.from_north(south)
        out = []
        for j in range(self.parts):
            s = slice(0, self.rows)
            total = self.storage[k, j, s, :] + west[j] + east[j] + south[j] + north[j]
            out.append(total + self.lower[k, j, s, :] + self.lower[k + 1, j, s, :])
        return out

    def sweep(self, src, dst, rhs, add, together):
        s = slice(0, self.rows)

        def body(k):
            def at(layer, j):
                return src[layer, j, s, :] if add is None else src[layer, j, s, :] + add(layer, j)

            now = [at(k, j) for j in range(self.parts)]
            west, south = self.load(self.west, k), self.load(self.south, k)
            w, b = self.from_west(now), self.from_south(now)
            e = self.from_east([p * q for p, q in zip(west, now)])
            f = self.from_north([p * q for p, q in zip(south, now)])
            for j in range(self.parts):
                total = rhs[k, j, s, :] + west[j] * w[j] + e[j] + south[j] * b[j] + f[j]
                total = total + self.lower[k, j, s, :] * at(below(k), j) + self.lower[k + 1, j, s, :] * at(above(k), j)
                dst[k, j, s, :] = (1.0 - OMEGA) * now[j] + self.gain[k, j, s, :] * total

        each_layer(body, together)

    def images(self, k, src, gravity=0.0, storage=True):
        s = slice(0, self.rows)
        now = self.load(src, k)
        west, south = self.load(self.west, k), self.load(self.south, k)
        w = [p * (v - n) for p, v, n in zip(west, now, self.from_west(now))]
        b = [p * (v - n) for p, v, n in zip(south, now, self.from_south(now))]
        e, f = self.from_east(w), self.from_north(b)
        out = []
        for j in range(self.parts):
            total = (w[j] - e[j]) + (b[j] - f[j])
            total = total + self.lower[k, j, s, :] * (now[j] - src[below(k), j, s, :] + gravity)
            total = total + self.lower[k + 1, j, s, :] * (now[j] - src[above(k), j, s, :] - gravity)
            if storage:
                total = total + self.storage[k, j, s, :] * now[j]
            out.append(total)
        return out


def restrict_to(fine, src, rhs, coarse, rhs_coarse, first, together):
    def body(k):
        images = fine.images(k, src)
        for j in range(coarse.parts):
            parts = [rhs[k, i, : fine.rows, :] - images[i] for i in range(4 * j, 4 * j + 4)]
            value = (parts[0] + parts[1]) + (parts[2] + parts[3])
            rhs_coarse[k, j, : fine.rows, :] = value
            first[k, j, : fine.rows, :] = coarse.gain[k, j, : fine.rows, :] * value

    each_layer(body, together)


def own_lanes(rows):
    lane = lanes_of(rows)
    return jnp.logical_and(lane >= BY // 4, lane < BY // 4 + BY // 2)


def strip_sums(fields):
    lane = lanes_of(SB, 128)
    out = jnp.zeros((SB, 128), F32)
    for i, field in enumerate(fields):
        for k in range(NZ):
            value = jnp.where(own_lanes(SB), field[k, :SB, :], 0.0)
            out = jnp.where(lane == 16 * i + k, 0.5 * jnp.sum(value, axis=1, keepdims=True), out)
    return out


def restrict_last(middle, src, rhs, rhs_last, together):
    def body(k):
        parts = [rhs[k, i, : middle.rows, :] - image for i, image in enumerate(middle.images(k, src))]
        rhs_last[k] = pair_sum(parts[0] + parts[1], 1)[:SB]

    each_layer(body, together)


def strip_pair(u):
    odd = (rows_of(u.shape[0], u.shape[1]) & 1) == 1
    return jnp.where(odd, row_roll(u, 1), row_roll(u, -1))


def coarsest(rhs, middle, south, lower, gain, sums, weight, out):
    num = sums + strip_pair(sums)
    den = weight + strip_pair(weight)
    mean = num / lane_roll(den, -16)

    lane = lanes_of(SB, 128)
    now = []
    for k in range(NZ):
        value = jnp.sum(jnp.where(lane == k, mean, 0.0), axis=1, keepdims=True)
        now.append(jnp.broadcast_to(value, (SB, LANES)))
    for _ in range(4):
        new = []
        for k in range(NZ):
            v, s = now[k], south[k]
            total = rhs[k] + s * lane_roll(v, 2) + lane_roll(s * v, -2) + middle[k] * strip_pair(v)
            total = total + lower[k] * now[below(k)] + lower[k + 1] * now[above(k)]
            new.append((1.0 - OMEGA) * v + gain[k] * total)
        now = new
    for k in range(NZ):
        out[k] = now[k]


def weights_of(sums):
    a, b, c, d, e, f = [sums[0:1, i : i + 1] for i in range(6)]
    beta2 = a + EPSILON
    beta = jnp.sqrt(beta2)
    kappa = (b + EPSILON) / beta2
    shift = EPSILON * (a - b) / beta2
    norm = kappa * shift - kappa * b + c
    h00 = (a - b) / beta2
    h10 = jnp.sqrt(jnp.maximum(norm, 0.0) / beta2 + EPSILON)
    scale = beta * h10
    scale2 = scale * scale
    h01 = (shift - kappa * b + d) / (beta * scale)
    h11 = (norm + kappa * (d + c - kappa * b) - e) / scale2
    p = kappa * (1.0 - h11) - h01 * h10
    q = h11 - 1.0 - kappa
    last = p * p * a + q * q * c + f + 2.0 * (p * q * b + p * d + q * e)
    h21_2 = jnp.maximum(last, 0.0) / scale2 + EPSILON
    g00 = h00 * h00 + h10 * h10
    g01 = h00 * h01 + h10 * h11
    g11 = h01 * h01 + h11 * h11 + h21_2
    r0 = beta * h00
    r1 = beta * h01
    factor = g01 / g00
    y1 = (r1 - factor * r0) / (g11 - factor * g01)
    y0 = (r0 - g01 * y1) / g00
    return y0 / beta + y1 * kappa / scale, -y1 / scale


def spread(field, left, right, first):
    lane = lanes_of(ROWS, 128)
    begin, end = lane < 32, lane >= 96
    tiles = []
    for odd in (0, 1):
        turn = 32 * odd + (0 if first else 64)
        low, high = (lane_roll(left, -turn), lane_roll(right, turn)) if turn else (left, right)
        tiles.append(jnp.where(begin, low, jnp.where(end, high, lane_roll(field, -32 if odd else 32))))
    return tiles


def put(ext, f, tiles):
    for half in (0, 1):
        ext[f, half, 0:ROWS, :] = tiles[half]
        ext[f, half, ROWS:, :] = tiles[half][0 : 4 * SA - ROWS]


def fetch(ext, f, j):
    return [ext[f, half, pl.ds(j, SA, stride=4), :] for half in (0, 1)]


def unpack_all(ext, cells, left, right, half, together):
    def unpack(f):
        put(ext, f, spread(cells(f), left(f), right(f), True))
        put(ext, f + half, spread(cells(f + half), left(f), right(f), False))

    each_layer(unpack, together, half)


def sorted_lanes(inverse=False):
    a, b = lanes_of(128), rows_of(128)
    if inverse:
        a, b = b, a
    return jnp.where(a == (b & 1) * 64 + (b >> 1), 1.0, 0.0).astype(F32)


def moved_lanes(field, matrix):
    rows = field.reshape(-1, 128)
    out = jnp.dot(rows, matrix, precision=lax.Precision.HIGHEST, preferred_element_type=F32)
    return out.reshape(field.shape)


def start_kernel(head_in, old_in, soil_in, recharge_in, tables, out, head, old, soil, recharge, sem):
    pairs = [(soil_in, soil), (old_in, old), (recharge_in, recharge), (head_in, head)]
    copies = [pltpu.make_async_copy(a, b, sem.at[i]) for i, (a, b) in enumerate(pairs)]
    for copy in copies:
        copy.start()
    matrix = sorted_lanes()
    copies[0].wait()
    out[0:NZ] = moved_lanes(soil[...].astype(F32), matrix)
    for copy in copies[1:]:
        copy.wait()
    base = []
    for k in range(NZ):
        porosity, resid = [jnp.take_along_axis(tables[i], soil[k], axis=1) for i in (2, 3)]
        value = porosity * (resid - old[k])
        base.append(value - recharge[...] if k == NZ - 1 else value)
    out[NZ : 2 * NZ] = moved_lanes(head[...], matrix)
    out[2 * NZ :] = moved_lanes(jnp.stack(base), matrix)


def soil_kernel(tables, cells, left, right, unread, *refs):
    (alpha, porous, hw, hs, hl), (ext, con) = refs[:5], refs[5:]
    unpack_all(ext, lambda f: cells[f], lambda f: left[f], lambda f: right[f], NZ // 2, 5)
    table = [jnp.concatenate([tables[i]] * (SA // 8), axis=0) for i in range(4)]

    def look_up(k):
        for j in range(4):
            for odd, tile in enumerate(fetch(ext, k, j)):
                kind = tile.astype(jnp.int32)
                con[k, 2 * j + odd], here, porosity, resid = [
                    jnp.take_along_axis(table[i], kind, axis=1) for i in range(4)
                ]
                alpha[k, 2 * j + odd] = here
                porous[k, 2 * j + odd] = porosity * (1.0 - resid)

    each_layer(look_up, 5)
    row = lax.axis_index("gx") * BX - REACH * BX + 4 * rows_of(SA)
    col = lax.axis_index("gy") * BY - BY // 2 + 2 * lanes_of(SA)
    edge_col = jnp.logical_or(col == 0, col == BY * lax.axis_size("gy"))
    edge_row = jnp.logical_or(row == 0, row == BX * lax.axis_size("gx"))

    def harmonic(k):
        inside = one_if(k != 0)
        for j in range(8):
            here = con[k, j]

            def face(there):
                return here * there / (here + there)

            west = face(con[k, j - 2]) if j > 1 else jnp.where(edge_row, 0.0, face(row_roll(con[k, 6 + j], 1)))
            south = face(con[k, j - 1]) if j % 2 else jnp.where(edge_col, 0.0, face(lane_roll(con[k, j + 1], 1)))
            hw[k, j] = west
            hs[k, j] = south
            hl[k, j] = inside * face(con[below(k), j])

    each_layer(harmonic, 5)


def fetch_kernel(*refs):
    stored, outs, sem = refs[:7], refs[8:15], refs[15]
    copies = [pltpu.make_async_copy(stored[i], outs[i], sem.at[i]) for i in range(7)]
    for copy in copies:
        copy.start()
    for copy in copies:
        copy.wait()


def setup_kernel(second, *refs):
    refs = list(refs)
    one, two, three = refs[:3]
    if second:
        statics, refs = refs[3:10], refs[10:]
    else:
        given, stored, refs = refs[3:8], refs[28:35], refs[8:28] + refs[35:]
        statics, sem = refs[27:29] + given, refs[29]
        copies = [pltpu.make_async_copy(statics[i], stored[i], sem.at[i]) for i in range(7)]
        for copy in copies[2:]:
            copy.start()
    head, base, alpha, porous, hw, hs, hl = statics
    (c0, w0, s0, l0, g0, b0, x0, c1, w1, s1, l1, g1, b1, x1, m2, s2, l2, g2, b2, sums) = refs[:20]
    ext, state, rel, x0a, x1a, c2, w2 = refs[20:27]
    if second:

        def rows(f):
            return jnp.concatenate([part[f] for part in (one, two, three)], axis=0)

        unpack_all(ext, rows, lambda f: rows(NZ + f), lambda f: rows(NZ + NZ // 2 + f), NZ // 2, 5)
    else:
        unpack_all(ext, lambda f: one[f], lambda f: two[f], lambda f: three[f], NZ, 5)

    def cells_of(k):
        for j in range(8):
            if j % 2 == 0:
                tiles = fetch(ext, k, j // 2)
                others = None if second else fetch(ext, NZ + k, j // 2)
            if second:
                moved = tiles[j % 2]
                here = head[k, j] + moved
                local = base[k, j] + STORAGE * moved
            else:
                here, local = tiles[j % 2], others[j % 2]
                head[k, j] = here
                base[k, j] = local
            effective = 1.0 / (1.0 + jnp.exp(-(alpha[k, j] * here)))
            state[k, j] = here
            rel[k, j] = effective * effective
            part = porous[k, j] * effective
            c0[k, j] = STORAGE + part * (alpha[k, j] * (1.0 - effective))
            b0[k, j] = local + part

    each_layer(cells_of, 10)
    if not second:
        for copy in copies[:2]:
            copy.start()

    fine = Level(c0, w0, s0, l0, g0, 4, 2, SA)
    mid = Level(c1, w1, s1, l1, g1, 2, 1, SA)

    def faces(k):
        wet = fine.load(rel, k)
        w, b = fine.from_west(wet), fine.from_south(wet)
        for j in range(8):
            w0[k, j] = hw[k, j] * (wet[j] + w[j])
            s0[k, j] = hs[k, j] * (wet[j] + b[j])
            l0[k, j] = hl[k, j] * (wet[j] + rel[below(k), j])

    each_layer(faces, 10)
    l0[NZ] = jnp.zeros((8, SA, LANES), F32)
    l1[NZ] = jnp.zeros((2, SA, LANES), F32)
    l2[NZ] = jnp.zeros((SB, LANES), F32)

    def residual(k):
        diagonals, images = fine.diagonals(k), fine.images(k, state, 1.0, False)
        for j in range(8):
            gain = OMEGA / diagonals[j]
            value = -(b0[k, j] + images[j])
            g0[k, j] = gain
            b0[k, j] = value
            x0a[k, j] = gain * value

    each_layer(residual, 5)

    def coarsen(k):
        for j in range(2):
            i = 4 * j
            c1[k, j] = (c0[k, i] + c0[k, i + 1]) + (c0[k, i + 2] + c0[k, i + 3])
            l1[k, j] = (l0[k, i] + l0[k, i + 1]) + (l0[k, i + 2] + l0[k, i + 3])
            w1[k, j] = w0[k, i] + w0[k, i + 1]
            s1[k, j] = s0[k, i] + s0[k, i + 2]

    each_layer(coarsen, 10)

    def coarse(k):
        for j, diagonal in enumerate(mid.diagonals(k)):
            g1[k, j] = OMEGA / diagonal
        c2[k] = pair_sum(c1[k, 0, :SB] + c1[k, 1, :SB], 1)
        l2[k] = pair_sum(l1[k, 0, :SB] + l1[k, 1, :SB], 1)
        w2[k] = pair_sum(w1[k, 0], 1)
        s2[k] = from_south(s1[k, 0, :SB] + s1[k, 1, :SB], 1)

    each_layer(coarse, 10)

    def coarse_gain(k):
        west = w2[k]
        east = row_roll(west, -1)[:SB]
        west = west[:SB]
        south = s2[k]
        diag = c2[k] + west + east + south + lane_roll(south, -2) + l2[k] + l2[k + 1]
        g2[k] = OMEGA / diag
        odd = (rows_of(SB) & 1) == 1
        m2[k] = jnp.where(odd, west, east)

    each_layer(coarse_gain, 10)
    fine.sweep(x0a, x0, b0, None, 10)
    restrict_to(fine, x0, b0, mid, b1, x1a, 5)
    mid.sweep(x1a, x1, b1, None, 10)
    restrict_last(mid, x1, b1, b2, 10)
    sums[...] = strip_sums([b2, c2])
    if not second:
        for copy in copies:
            copy.wait()


def finish(fine, mid, last, b0, x0, b1, x1, b2, sums, weight, work0, work1, e2):
    m2, s2, l2, g2 = last
    coarsest(b2, m2, s2, l2, g2, sums, weight, e2)
    mid.sweep(x1, work1[0], b1, lambda k, j: e2[k], 10)
    mid.sweep(work1[0], work1[1], b1, None, 10)
    corrected = work1[1]
    fine.sweep(x0, work0[0], b0, lambda k, j: corrected[k, j // 4, : fine.rows, :], 10)
    fine.sweep(work0[0], work0[1], b0, None, 10)
    return work0[1]


def write_own(dst, k, j, even, odd):
    lane = lanes_of(8, 128)
    s = slice(OWN_S, OWN_S + 8)
    own = jnp.where(lane < 64, lane_roll(even[s], -32), lane_roll(odd[s], 32))
    for half in (0, 1):
        dst[k, 4 * half + j : 4 * half + j + 1, :] = own[half : half + 1]


def cycle_kernel(
    total, weight, c0, w0, s0, l0, g0, b0, x0, c1, w1, s1, l1, g1, b1, x1, m2, s2, l2, g2, b2,
    r0, y0, r1, y1, r2, sums, move,
    f0, f1, h0, h1, e2,
):
    fine = Level(c0, w0, s0, l0, g0, 4, 2, SB)
    mid = Level(c1, w1, s1, l1, g1, 2, 1, SB)
    z = finish(
        fine, mid, (m2, s2, l2, g2), b0, x0, b1, x1, b2, total[...], weight[...], (f0, f1), (h0, h1), e2
    )

    def residual(k):
        images = fine.images(k, z)
        for j in range(8):
            value = b0[k, j, :SB, :] - images[j]
            r0[k, j] = value
            f0[k, j] = g0[k, j, :SB, :] * value
        for j in range(4):
            write_own(move, k, j, z[k, 2 * j], z[k, 2 * j + 1])

    each_layer(residual, 5)
    fine.sweep(f0, y0, r0, None, 10)
    restrict_to(fine, y0, r0, mid, r1, h0, 5)
    mid.sweep(h0, y1, r1, None, 10)
    restrict_last(mid, y1, r1, r2, 10)
    sums[...] = strip_sums([r2])


def last_kernel(
    total, weight, c0, w0, s0, l0, g0, start, c1, w1, s1, l1, g1, m2, s2, l2, g2, b0, x0, b1, x1, b2,
    products, move,
    f0, f1, h0, h1, e2,
):
    fine = Level(c0, w0, s0, l0, g0, 4, 2, SB)
    mid = Level(c1, w1, s1, l1, g1, 2, 1, SB)
    z = finish(
        fine, mid, (m2, s2, l2, g2), b0, x0, b1, x1, b2, total[...], weight[...], (f0, f1), (h0, h1), e2
    )
    row = rows_of(8)
    own = jnp.logical_and(own_lanes(8), row < 2)

    def body(k, sums):
        sums = list(sums)
        images = fine.images(k, z)
        for j in range(4):
            write_own(move, k, j, z[k, 2 * j], z[k, 2 * j + 1])
        for j in range(8):
            image = images[j][OWN_S : OWN_S + 8]
            u = jnp.where(own, start[k, j, OWN_S : OWN_S + 8, :], 0.0)
            t = jnp.where(own, b0[k, j, OWN_S : OWN_S + 8, :], 0.0)
            r = jnp.where(own, t - image, 0.0)
            for i, item in enumerate((u * u, u * t, t * t, u * r, t * r, r * r)):
                sums[i] = sums[i] + item
        return tuple(sums)

    sums = (jnp.zeros((8, LANES), F32),) * 6
    for k in range(NZ):
        sums = body(k, sums)
    lane = lanes_of(1, 128)
    out = jnp.zeros((1, 128), F32)
    for i, item in enumerate(sums):
        value = jnp.sum(jnp.sum(item, axis=0, keepdims=True), axis=1, keepdims=True)
        out = jnp.where(lane == i, value, out)
    products[...] = out


def move_kernel(products, first, second, out):
    one, two = weights_of(products)
    out[...] = one[None] * first[...] + two[None] * second[...]


def end_kernel(head, moved, products, first, second, out):
    one, two = weights_of(products)
    change = moved[...] + one[None] * first[...] + two[None] * second[...]
    out[...] = head[...] + moved_lanes(change, sorted_lanes(True))


VMEM = pl.BlockSpec(memory_space=pltpu.VMEM)
HBM = pl.BlockSpec(memory_space=pltpu.HBM)


def shape(*dims):
    return jax.ShapeDtypeStruct(dims, F32)


def buffer(*dims):
    return pltpu.VMEM(dims, F32)


ANY = pl.BlockSpec(memory_space=pl.ANY)


def call(kernel, args, outs, scratch, limit, in_hbm=(), out_hbm=(), unread=(), cost=None):
    place = [ANY if i in unread else HBM if i in in_hbm else VMEM for i in range(len(args))]
    args = [pltpu.with_memory_space_constraint(a, pltpu.HBM) if i in in_hbm else a for i, a in enumerate(args)]
    many = isinstance(outs, list)
    if many:
        outs = [pltpu.HBM(a.shape, a.dtype) if i in out_hbm else a for i, a in enumerate(outs)]
    spec = [HBM if i in out_hbm else VMEM for i in range(len(outs))] if many else VMEM
    return pl.pallas_call(
        kernel,
        out_shape=outs,
        in_specs=place,
        out_specs=spec,
        scratch_shapes=scratch,
        compiler_params=pltpu.CompilerParams(vmem_limit_bytes=limit),
        cost_estimate=cost,
    )(*args)


FINE = (NZ, 8, SA, LANES)


def soil_fields(inputs):
    cost = pl.CostEstimate(flops=10**7, bytes_accessed=2 * 10**7, transcendentals=0)
    scratch = [buffer(NZ, 2, 4 * SA, 128), buffer(*FINE)]
    return call(soil_kernel, inputs, [shape(*FINE)] * 5, scratch, 6 << 20, unread=(4,), cost=cost)


def fetched(stored, after):
    cost = pl.CostEstimate(flops=10**6, bytes_accessed=15 * 10**6, transcendentals=0)
    sem = [pltpu.SemaphoreType.DMA((7,))]
    return call(fetch_kernel, [*stored, after], [shape(*FINE)] * 7, sem, 1 << 20, range(7), unread=(7,), cost=cost)


def setup(inputs, second):
    fine = shape(*FINE)
    outs = (
        [fine] * 3 + [shape(NZ + 1, 8, SA, LANES)] + [fine] * 3
        + [shape(NZ, 2, SA, LANES)] * 3 + [shape(NZ + 1, 2, SA, LANES)] + [shape(NZ, 2, SA, LANES)] * 3
        + [shape(NZ, SB, LANES)] * 2 + [shape(NZ + 1, SB, LANES)] + [shape(NZ, SB, LANES)] * 2
        + [shape(SB, 128)] + ([] if second else [fine] * 7)
    )
    scratch = (
        [buffer(NZ if second else 2 * NZ, 2, 4 * SA, 128)] + [buffer(*FINE)] * 3
        + [buffer(NZ, 2, SA, LANES), buffer(NZ, SB, LANES), buffer(NZ, SA, LANES)]
        + ([] if second else [buffer(*FINE)] * 2 + [pltpu.SemaphoreType.DMA((7,))])
    )
    kernel = functools.partial(setup_kernel, second)
    return call(kernel, inputs, outs, scratch, (8 if second else 11) << 20, (), () if second else range(20, 27))


def work():
    return [buffer(NZ, 8, SB, LANES)] * 2 + [buffer(NZ, 2, SB, LANES)] * 2 + [buffer(NZ, SB, LANES)]


def shifted(field, axis, by):
    count = lax.axis_size(axis)
    return lax.ppermute(field, axis, [(i, (i + by) % count) for i in range(count)])


def wider(near):
    return shifted(near, "gx", 3), near, shifted(near, "gx", -3)


def pack_kernel(west, near, east, *refs):
    rows, to_north, to_south = refs[-3:]
    half = rows.shape[0] // 2
    lane = lanes_of(rows.shape[1], 128)

    def quarters(*parts):
        return jnp.where(lane < 64, jnp.where(lane < 32, *parts[:2]), jnp.where(lane < 96, *parts[2:]))

    def pack(f):
        low, high = [
            jnp.concatenate([part[i] for part in (west, near, east)], axis=0) for i in (f, f + half)
        ]
        rows[f] = low
        rows[f + half] = high
        to_north[f] = quarters(lane_roll(low, -32), lane_roll(low, -64), lane_roll(high, 32), high)
        to_south[f] = quarters(lane_roll(high, -64), lane_roll(high, 32), low, lane_roll(low, 96))

    each_layer(pack, 5, half)


def packed(parts, after=()):
    fields, rows = parts[0].shape[0], 3 * parts[0].shape[1]
    outs = [shape(fields, rows, BY)] + [shape(fields // 2, rows, BY)] * 2
    return call(pack_kernel, [*parts, *after], outs, [], 4 << 20, unread=range(3, 3 + len(after)))


def sideways(packs):
    rows, to_north, to_south = packs
    return rows, shifted(to_north, "gy", 1), shifted(to_south, "gy", -1)


def around(field):
    full = jnp.concatenate(sideways(packed((shifted(field, "gx", 1), field, shifted(field, "gx", -1)))), axis=0)
    return shifted(full, "gx", 3), full, shifted(full, "gx", -3)


def summed(field):
    count = lax.axis_size("gy")
    for flip in (1, 2, 6):
        if flip < count:
            field = field + lax.ppermute(field, "gy", [(i, i ^ flip) for i in range(count)])
    return field


def summed_over_all(row):
    axes = ("gx", "gy")
    count = lax.axis_size(axes)
    parts = lax.all_to_all(jnp.broadcast_to(row[None], (count, 1, 128)), axes, 0, 0, tiled=True)
    return jnp.sum(parts, axis=0)


def on_device(
    pressure, saturation_old, soil_type, recharge, ksat_table, alpha_table, porosity_table, residual_table
):
    tables = jnp.stack([ksat_table, alpha_table, porosity_table, residual_table])
    tables = jnp.pad(tables, ((0, 0), (0, 128 - tables.shape[1])))
    tables = jnp.broadcast_to(tables[:, None, :], (4, 8, 128))
    block = (NZ, BX, BY)
    start = call(
        start_kernel,
        [pressure, saturation_old, soil_type, recharge, tables],
        shape(3 * NZ, BX, BY),
        [buffer(*block), buffer(*block), pltpu.VMEM(block, jnp.int32), buffer(BX, BY), pltpu.SemaphoreType.DMA((4,))],
        4 << 20,
        range(4),
    )
    near = jnp.concatenate([shifted(start, "gx", 1), start, shifted(start, "gx", -1)], axis=1)
    soil_cells = sideways(packed(wider(near[:NZ])))
    packs = packed(wider(near[NZ:]), soil_cells[1:])
    cells = sideways(packs)
    given = soil_fields([tables, *soil_cells, packs[1]])
    moved = None
    for newton in range(2):
        if newton:
            parts = around(moved)
            got = setup([*parts, *fetched(stored, parts[1])], True)
        else:
            got = setup([*cells, *given], False)
            stored = got[20:]
        (c0, w0, s0, l0, g0, b0, x0, c1, w1, s1, l1, g1, b1, x1, m2, s2, l2, g2, b2, sums) = got[:20]
        weight = summed(sums)
        r0, y0, r1, y1, r2, sums, first = call(
            cycle_kernel,
            [weight, weight, *got[:19]],
            [shape(NZ, 8, SB, LANES)] * 2 + [shape(NZ, 2, SB, LANES)] * 2
            + [shape(NZ, SB, LANES), shape(SB, 128), shape(NZ, BX, BY)],
            work(),
            6 << 20,
        )
        total = summed(sums)
        products, second = call(
            last_kernel,
            [total, weight, c0, w0, s0, l0, g0, b0, c1, w1, s1, l1, g1, m2, s2, l2, g2, r0, y0, r1, y1, r2],
            [shape(1, 128), shape(NZ, BX, BY)],
            work(),
            6 << 20,
        )
        ends = [summed_over_all(products), first, second]
        if newton:
            return call(end_kernel, [pressure, moved, *ends], shape(NZ, BX, BY), [], 4 << 20)
        moved = call(move_kernel, ends, shape(NZ, BX, BY), [], 4 << 20)


def solution(mesh):
    placed = (P(None, "gx", "gy"),) * 3 + (P("gx", "gy"),) + (P(),) * 4
    return jax.shard_map(
        on_device, mesh=mesh, in_specs=placed, out_specs=P(None, "gx", "gy"), check_vma=False
    )
```

profile of v0, /device:TPU:1, one launch (start us, length us, event | category | flops | bytes accessed | tf_op | source)
XLA Modules:
  0.0 171.6 jit_solution(11957121196934511284)
XLA Ops:
  2.1 8.7 %collective-permute-start.1 = (f32[30,8,128]{2,1,0:T(8,128)S(1)}, f32[30,8,128]{2,1,0:T(8,128)S(1)}, u32[]{:S(2)}, u32[]{:S(2)}) collective-permute-start(f32[30,8,128]{2,1,0:T(8,128)S(1)} %shard_map.82), channel_id=1, source_target_pairs={{0,248},{8,0},{16,8},{24,16},{32,24},{40,32},{48,40},{56,48},{64,5... | collective-permute-start | bytes 368648 | tf_op jit(solution)/shard_map/ppermute | solution.py:631
  10.7 1.9 %collective-permute-done.1 = f32[30,8,128]{2,1,0:T(8,128)S(1)} collective-permute-done((f32[30,8,128]{2,1,0:T(8,128)S(1)}, f32[30,8,128]{2,1,0:T(8,128)S(1)}, u32[]{:S(2)}, u32[]{:S(2)}) %collective-permute-start.1) | collective-permute-done | bytes 122912 | tf_op jit(solution)/shard_map/ppermute | solution.py:631
  12.6 5.2 %collective-permute-done = f32[30,8,128]{2,1,0:T(8,128)S(1)} collective-permute-done((f32[30,8,128]{2,1,0:T(8,128)S(1)}, f32[30,8,128]{2,1,0:T(8,128)S(1)}, u32[]{:S(2)}, u32[]{:S(2)}) %collective-permute-start) | collective-permute-done | bytes 122912 | tf_op jit(solution)/shard_map/ppermute | solution.py:631
  17.9 2.7 %collective-permute-start.4 = (f32[10,24,128]{2,1,0:T(8,128)S(1)}, f32[10,24,128]{2,1,0:T(8,128)S(1)}, u32[]{:S(2)}, u32[]{:S(2)}) collective-permute-start(f32[10,24,128]{2,1,0:T(8,128)S(1)} %pad_maximum_fusion.1.near), channel_id=1, source_target_pairs={{0,24},{8,32},{16,40},{24,48},{32,56},{40,64},{48,72},{56,80},{64,... | collective-permute-start | bytes 368648 | tf_op jit(solution)/shard_map/ppermute | solution.py:631
  24.1 4.6 %collective-permute-start.6 = (f32[5,72,128]{2,1,0:T(8,128)S(1)}, f32[5,72,128]{2,1,0:T(8,128)S(1)}, u32[]{:S(2)}, u32[]{:S(2)}) collective-permute-start(f32[5,72,128]{2,1,0:T(8,128)S(1)} %get-tuple-element.91), channel_id=1, source_target_pairs={{0,1},{1,2},{2,3},{3,4},{4,5},{5,6},{6,7},{7,0},{8,9},{9,10},{10,1... | collective-permute-start | bytes 552968 | tf_op jit(solution)/shard_map/ppermute | solution.py:631
  29.0 2.2 %collective-permute-done.6.refs_0_.left = f32[5,72,128]{2,1,0:T(8,128)S(1)} collective-permute-done((f32[5,72,128]{2,1,0:T(8,128)S(1)}, f32[5,72,128]{2,1,0:T(8,128)S(1)}, u32[]{:S(2)}, u32[]{:S(2)}) %collective-permute-start.6) | collective-permute-done | bytes 184352 | tf_op jit(solution)/shard_map/ppermute | solution.py:631
  31.2 2.5 %collective-permute-done.7.refs_1_.right = f32[5,72,128]{2,1,0:T(8,128)S(1)} collective-permute-done((f32[5,72,128]{2,1,0:T(8,128)S(1)}, f32[5,72,128]{2,1,0:T(8,128)S(1)}, u32[]{:S(2)}, u32[]{:S(2)}) %collective-permute-start.7) | collective-permute-done | bytes 184352 | tf_op jit(solution)/shard_map/ppermute | solution.py:631
  35.9 3.6 %shard_map.85 = (f32[10,8,24,128]{3,2,1,0:T(8,128)S(1)}, f32[10,8,24,128]{3,2,1,0:T(8,128)S(1)}, f32[10,8,24,128]{3,2,1,0:T(8,128)S(1)}, f32[10,8,24,128]{3,2,1,0:T(8,128)S(1)}, f32[10,8,24,128]{3,2,1,0:T(8,128)S(1)}) custom-call(f32[4,8,128]{2,1,0:T(8,128)S(1)} %broadcast_in_dim.10.tables, f32[10,72,128]{2,1,0:T(8,128)S(1)} %get-tuple-element.96.cells, ...), custom_call_target="tpu_custom_call" | custom-call | flops 10000000 | bytes 20000000 | tf_op jit(solution)/shard_map/pallas_call | solution.py:582
  41.4 5.2 %shard_map.86 = (f32[10,8,24,128]{3,2,1,0:T(8,128)S(1)}, f32[10,8,24,128]{3,2,1,0:T(8,128)S(1)}, f32[10,8,24,128]{3,2,1,0:T(8,128)S(1)}, f32[11,8,24,128]{3,2,1,...) custom-call(f32[20,72,128]{2,1,0:T(8,128)S(1)} %get-tuple-element.93, ...), custom_call_target="tpu_custom_call" | custom-call | tf_op jit(solution)/shard_map/pallas_call | solution.py:582
  46.6 4.0 %collective-permute-start.10 = (f32[16,128]{1,0:T(8,128)S(1)}, f32[16,128]{1,0:T(8,128)S(1)}, u32[]{:S(2)}, u32[]{:S(2)}) collective-permute-start(f32[16,128]{1,0:T(8,128)S(1)} %get-tuple-element.102), channel_id=1, source_target_pairs={{0,1},{1,0},{2,3},{3,2},{4,5},{5,4},{6,7},{7,6},{8,9},{9,8},{10,11... | collective-permute-start | bytes 24584 | tf_op jit(solution)/shard_map/ppermute | solution.py:678
  51.5 2.5 %collective-permute-done.11 = f32[16,128]{1,0:T(8,128)S(1)} collective-permute-done((f32[16,128]{1,0:T(8,128)S(1)}, f32[16,128]{1,0:T(8,128)S(1)}, u32[]{:S(2)}, u32[]{:S(2)}) %collective-permute-start.11) | collective-permute-done | bytes 8224 | tf_op jit(solution)/shard_map/ppermute | solution.py:678
  54.0 3.7 %collective-permute-done.12 = f32[16,128]{1,0:T(8,128)S(1)} collective-permute-done((f32[16,128]{1,0:T(8,128)S(1)}, f32[16,128]{1,0:T(8,128)S(1)}, u32[]{:S(2)}, u32[]{:S(2)}) %collective-permute-start.12) | collective-permute-done | bytes 8224 | tf_op jit(solution)/shard_map/ppermute | solution.py:678
  57.7 3.9 %shard_map.87 = (f32[10,8,16,128]{3,2,1,0:T(8,128)S(1)}, f32[10,8,16,128]{3,2,1,0:T(8,128)S(1)}, f32[10,2,16,128]{3,2,1,0:T(8,128)S(1)}, f32[10,2,16,128]{3,2,1,...) custom-call(f32[16,128]{1,0:T(8,128)S(1)} %add.40.total.weight, ...), custom_call_target="tpu_custom_call" | custom-call | tf_op jit(solution)/shard_map/pallas_call | solution.py:582
  61.5 2.7 %collective-permute-start.13 = (f32[16,128]{1,0:T(8,128)S(1)}, f32[16,128]{1,0:T(8,128)S(1)}, u32[]{:S(2)}, u32[]{:S(2)}) collective-permute-start(f32[16,128]{1,0:T(8,128)S(1)} %get-tuple-element.122), channel_id=1, source_target_pairs={{0,1},{1,0},{2,3},{3,2},{4,5},{5,4},{6,7},{7,6},{8,9},{9,8},{10,11... | collective-permute-start | bytes 24584 | tf_op jit(solution)/shard_map/ppermute | solution.py:678
  65.1 2.5 %collective-permute-done.14 = f32[16,128]{1,0:T(8,128)S(1)} collective-permute-done((f32[16,128]{1,0:T(8,128)S(1)}, f32[16,128]{1,0:T(8,128)S(1)}, u32[]{:S(2)}, u32[]{:S(2)}) %collective-permute-start.14) | collective-permute-done | bytes 8224 | tf_op jit(solution)/shard_map/ppermute | solution.py:678
  67.6 3.7 %collective-permute-done.15 = f32[16,128]{1,0:T(8,128)S(1)} collective-permute-done((f32[16,128]{1,0:T(8,128)S(1)}, f32[16,128]{1,0:T(8,128)S(1)}, u32[]{:S(2)}, u32[]{:S(2)}) %collective-permute-start.15) | collective-permute-done | bytes 8224 | tf_op jit(solution)/shard_map/ppermute | solution.py:678
  71.3 2.2 %shard_map.88 = (f32[1,128]{1,0:T(1,128)S(1)}, f32[10,8,128]{2,1,0:T(8,128)S(1)}) custom-call(f32[16,128]{1,0:T(8,128)S(1)} %add.43.total, f32[16,128]{1,0:T(8,128)S(1)} %add.40.total.weight, f32[10,8,24,128]{3,2,1,0:T(8,128)S(1)} %get-tuple-element.103.c0, f32[10,8,24,128]{3,2,1,0:T(8,128)S(1)} %get-tuple-element.104.w0, ...), custom_call_target="tpu_custom_call" | custom-call | tf_op jit(solution)/shard_map/pallas_call | solution.py:582
  73.7 21.6 %all_to_all.10 = f32[256,1,128]{2,1,0:T(1,128)S(1)} all-to-all(f32[256,1,128]{2,1,0:T(1,128)S(1)} %broadcast_in_dim.24), channel_id=1, replica_groups=mesh['gx'=32,'gy'=8] {'gx','gy'}, dimensions={0} | all-to-all | bytes 262144 | tf_op jit(solution)/shard_map/all_to_all | solution.py:685
  98.7 4.2 %collective-permute-done.16.west = f32[10,8,128]{2,1,0:T(8,128)S(1)} collective-permute-done((f32[10,8,128]{2,1,0:T(8,128)S(1)}, f32[10,8,128]{2,1,0:T(8,128)S(1)}, u32[]{:S(2)}, u32[]{:S(2)}) %collective-permute-start.16) | collective-permute-done | bytes 40992 | tf_op jit(solution)/shard_map/ppermute | solution.py:631
  106.1 2.6 %collective-permute-done.19 = f32[5,24,128]{2,1,0:T(8,128)S(1)} collective-permute-done((f32[5,24,128]{2,1,0:T(8,128)S(1)}, f32[5,24,128]{2,1,0:T(8,128)S(1)}, u32[]{:S(2)}, u32[]{:S(2)}) %collective-permute-start.19) | collective-permute-done | bytes 61472 | tf_op jit(solution)/shard_map/ppermute | solution.py:631
  108.8 2.7 %collective-permute-start.20 = (f32[20,24,128]{2,1,0:T(8,128)S(1)}, f32[20,24,128]{2,1,0:T(8,128)S(1)}, u32[]{:S(2)}, u32[]{:S(2)}) collective-permute-start(f32[20,24,128]{2,1,0:T(8,128)S(1)} %constant_dynamic-update-slice_fusion.refs_7_.refs_1_), channel_id=1, source_target_pairs={{0,24},{8,32},{16,40},{24,48},{32,56},{40,64},{48,72},{56,80},{64,... | collective-permute-start | bytes 737288 | tf_op jit(solution)/shard_map/ppermute | solution.py:631
  111.4 3.0 %shard_map.91 = (f32[10,8,24,128]{3,2,1,0:T(8,128)S(1)}, f32[10,8,24,128]{3,2,1,0:T(8,128)S(1)}, f32[10,8,24,128]{3,2,1,0:T(8,128)S(1)}, f32[10,8,24,128]{3,2,1,...) custom-call(f32[10,8,24,128]{3,2,1,0:T(8,128)} %get-tuple-element.134, ...), custom_call_target="tpu_custom_call" | custom-call | flops 1000000 | bytes 15000000 | tf_op jit(solution)/shard_map/pallas_call | solution.py:582
  117.5 4.7 %shard_map.92 = (f32[10,8,24,128]{3,2,1,0:T(8,128)S(1)}, f32[10,8,24,128]{3,2,1,0:T(8,128)S(1)}, f32[10,8,24,128]{3,2,1,0:T(8,128)S(1)}, f32[11,8,24,128]{3,2,1,...) custom-call(f32[20,24,128]{2,1,0:T(8,128)S(1)} %collective-permute-d, ...), custom_call_target="tpu_custom_call" | custom-call | tf_op jit(solution)/shard_map/pallas_call | solution.py:582
  122.2 2.1 %collective-permute-start.22 = (f32[16,128]{1,0:T(8,128)S(1)}, f32[16,128]{1,0:T(8,128)S(1)}, u32[]{:S(2)}, u32[]{:S(2)}) collective-permute-start(f32[16,128]{1,0:T(8,128)S(1)} %get-tuple-element.148), channel_id=1, source_target_pairs={{0,1},{1,0},{2,3},{3,2},{4,5},{5,4},{6,7},{7,6},{8,9},{9,8},{10,11... | collective-permute-start | bytes 24584 | tf_op jit(solution)/shard_map/ppermute | solution.py:678
  125.1 2.5 %collective-permute-done.23 = f32[16,128]{1,0:T(8,128)S(1)} collective-permute-done((f32[16,128]{1,0:T(8,128)S(1)}, f32[16,128]{1,0:T(8,128)S(1)}, u32[]{:S(2)}, u32[]{:S(2)}) %collective-permute-start.23) | collective-permute-done | bytes 8224 | tf_op jit(solution)/shard_map/ppermute | solution.py:678
  128.8 2.5 %collective-permute-done.24 = f32[16,128]{1,0:T(8,128)S(1)} collective-permute-done((f32[16,128]{1,0:T(8,128)S(1)}, f32[16,128]{1,0:T(8,128)S(1)}, u32[]{:S(2)}, u32[]{:S(2)}) %collective-permute-start.24) | collective-permute-done | bytes 8224 | tf_op jit(solution)/shard_map/ppermute | solution.py:678
  131.4 4.1 %shard_map.93 = (f32[10,8,16,128]{3,2,1,0:T(8,128)S(1)}, f32[10,8,16,128]{3,2,1,0:T(8,128)S(1)}, f32[10,2,16,128]{3,2,1,0:T(8,128)S(1)}, f32[10,2,16,128]{3,2,1,...) custom-call(f32[16,128]{1,0:T(8,128)S(1)} %add.46.total.weight, ...), custom_call_target="tpu_custom_call" | custom-call | tf_op jit(solution)/shard_map/pallas_call | solution.py:582
  135.5 2.7 %collective-permute-start.25 = (f32[16,128]{1,0:T(8,128)S(1)}, f32[16,128]{1,0:T(8,128)S(1)}, u32[]{:S(2)}, u32[]{:S(2)}) collective-permute-start(f32[16,128]{1,0:T(8,128)S(1)} %get-tuple-element.168), channel_id=1, source_target_pairs={{0,1},{1,0},{2,3},{3,2},{4,5},{5,4},{6,7},{7,6},{8,9},{9,8},{10,11... | collective-permute-start | bytes 24584 | tf_op jit(solution)/shard_map/ppermute | solution.py:678
  139.1 2.5 %collective-permute-done.26 = f32[16,128]{1,0:T(8,128)S(1)} collective-permute-done((f32[16,128]{1,0:T(8,128)S(1)}, f32[16,128]{1,0:T(8,128)S(1)}, u32[]{:S(2)}, u32[]{:S(2)}) %collective-permute-start.26) | collective-permute-done | bytes 8224 | tf_op jit(solution)/shard_map/ppermute | solution.py:678
  142.6 2.7 %collective-permute-done.27 = f32[16,128]{1,0:T(8,128)S(1)} collective-permute-done((f32[16,128]{1,0:T(8,128)S(1)}, f32[16,128]{1,0:T(8,128)S(1)}, u32[]{:S(2)}, u32[]{:S(2)}) %collective-permute-start.27) | collective-permute-done | bytes 8224 | tf_op jit(solution)/shard_map/ppermute | solution.py:678
  145.3 2.4 %shard_map.94 = (f32[1,128]{1,0:T(1,128)S(1)}, f32[10,8,128]{2,1,0:T(8,128)S(1)}) custom-call(f32[16,128]{1,0:T(8,128)S(1)} %add.49.total, f32[16,128]{1,0:T(8,128)S(1)} %add.46.total.weight, f32[10,8,24,128]{3,2,1,0:T(8,128)S(1)} %get-tuple-element.149.c0, f32[10,8,24,128]{3,2,1,0:T(8,128)S(1)} %get-tuple-element.150.w0, ...), custom_call_target="tpu_custom_call" | custom-call | tf_op jit(solution)/shard_map/pallas_call | solution.py:582
  147.7 22.5 %all_to_all.11 = f32[256,1,128]{2,1,0:T(1,128)S(1)} all-to-all(f32[256,1,128]{2,1,0:T(1,128)S(1)} %broadcast_in_dim.26), channel_id=1, replica_groups=mesh['gx'=32,'gy'=8] {'gx','gy'}, dimensions={0} | all-to-all | bytes 262144 | tf_op jit(solution)/shard_map/all_to_all | solution.py:685
  (66 shorter events, 26.9 us)
Async XLA Ops:
  2.1 10.6 %collective-permute-start.1 = (f32[30,8,128]{2,1,0:T(8,128)S(1)}, f32[30,8,128]{2,1,0:T(8,128)S(1)}, u32[]{:S(2)}, u32[]{:S(2)}) collective-permute-start(f32[30,8,128]{2,1,0:T(8,128)S(1)} %shard_map.82), channel_id=1, source_target_pairs={{0,248},{8,0},{16,8},{24,16},{32,24},{40,32},{48,40},{56,48},{64,5... | collective-permute-start | bytes 368648 | tf_op jit(solution)/shard_map/ppermute | solution.py:631
  10.7 7.1 %collective-permute-start = (f32[30,8,128]{2,1,0:T(8,128)S(1)}, f32[30,8,128]{2,1,0:T(8,128)S(1)}, u32[]{:S(2)}, u32[]{:S(2)}) collective-permute-start(f32[30,8,128]{2,1,0:T(8,128)S(1)} %shard_map.82), channel_id=1, source_target_pairs={{0,8},{8,16},{16,24},{24,32},{32,40},{40,48},{48,56},{56,64},{64,7... | collective-permute-start | bytes 368648 | tf_op jit(solution)/shard_map/ppermute | solution.py:631
  17.8 5.6 %collective-permute-start.5 = (f32[10,24,128]{2,1,0:T(8,128)S(1)}, f32[10,24,128]{2,1,0:T(8,128)S(1)}, u32[]{:S(2)}, u32[]{:S(2)}) collective-permute-start(f32[10,24,128]{2,1,0:T(8,128)S(1)} %pad_maximum_fusion.1.near), channel_id=1, source_target_pairs={{0,232},{8,240},{16,248},{24,0},{32,8},{40,16},{48,24},{56,32},{64... | collective-permute-start | bytes 368648 | tf_op jit(solution)/shard_map/ppermute | solution.py:631
  17.9 5.9 %collective-permute-start.4 = (f32[10,24,128]{2,1,0:T(8,128)S(1)}, f32[10,24,128]{2,1,0:T(8,128)S(1)}, u32[]{:S(2)}, u32[]{:S(2)}) collective-permute-start(f32[10,24,128]{2,1,0:T(8,128)S(1)} %pad_maximum_fusion.1.near), channel_id=1, source_target_pairs={{0,24},{8,32},{16,40},{24,48},{32,56},{40,64},{48,72},{56,80},{64,... | collective-permute-start | bytes 368648 | tf_op jit(solution)/shard_map/ppermute | solution.py:631
  20.6 8.2 %collective-permute-start.3 = (f32[20,24,128]{2,1,0:T(8,128)S(1)}, f32[20,24,128]{2,1,0:T(8,128)S(1)}, u32[]{:S(2)}, u32[]{:S(2)}) collective-permute-start(f32[20,24,128]{2,1,0:T(8,128)S(1)} %slice.8.near), channel_id=1, source_target_pairs={{0,232},{8,240},{16,248},{24,0},{32,8},{40,16},{48,24},{56,32},{64... | collective-permute-start | bytes 737288 | tf_op jit(solution)/shard_map/ppermute | solution.py:631
  21.7 7.3 %collective-permute-start.2 = (f32[20,24,128]{2,1,0:T(8,128)S(1)}, f32[20,24,128]{2,1,0:T(8,128)S(1)}, u32[]{:S(2)}, u32[]{:S(2)}) collective-permute-start(f32[20,24,128]{2,1,0:T(8,128)S(1)} %slice.8.near), channel_id=1, source_target_pairs={{0,24},{8,32},{16,40},{24,48},{32,56},{40,64},{48,72},{56,80},{64,... | collective-permute-start | bytes 737288 | tf_op jit(solution)/shard_map/ppermute | solution.py:631
  24.1 7.1 %collective-permute-start.6 = (f32[5,72,128]{2,1,0:T(8,128)S(1)}, f32[5,72,128]{2,1,0:T(8,128)S(1)}, u32[]{:S(2)}, u32[]{:S(2)}) collective-permute-start(f32[5,72,128]{2,1,0:T(8,128)S(1)} %get-tuple-element.91), channel_id=1, source_target_pairs={{0,1},{1,2},{2,3},{3,4},{4,5},{5,6},{6,7},{7,0},{8,9},{9,10},{10,1... | collective-permute-start | bytes 552968 | tf_op jit(solution)/shard_map/ppermute | solution.py:631
  28.7 5.0 %collective-permute-start.7 = (f32[5,72,128]{2,1,0:T(8,128)S(1)}, f32[5,72,128]{2,1,0:T(8,128)S(1)}, u32[]{:S(2)}, u32[]{:S(2)}) collective-permute-start(f32[5,72,128]{2,1,0:T(8,128)S(1)} %get-tuple-element.92), channel_id=1, source_target_pairs={{0,7},{1,0},{2,1},{3,2},{4,3},{5,4},{6,5},{7,6},{8,15},{9,8},{10,9... | collective-permute-start | bytes 552968 | tf_op jit(solution)/shard_map/ppermute | solution.py:631
  34.2 7.2 %collective-permute-start.9 = (f32[10,72,128]{2,1,0:T(8,128)S(1)}, f32[10,72,128]{2,1,0:T(8,128)S(1)}, u32[]{:S(2)}, u32[]{:S(2)}) collective-permute-start(f32[10,72,128]{2,1,0:T(8,128)S(1)} %get-tuple-element.95), channel_id=1, source_target_pairs={{0,7},{1,0},{2,1},{3,2},{4,3},{5,4},{6,5},{7,6},{8,15},{9,8},{10,9... | collective-permute-start | bytes 1105928 | tf_op jit(solution)/shard_map/ppermute | solution.py:631
  34.2 7.2 %collective-permute-start.8 = (f32[10,72,128]{2,1,0:T(8,128)S(1)}, f32[10,72,128]{2,1,0:T(8,128)S(1)}, u32[]{:S(2)}, u32[]{:S(2)}) collective-permute-start(f32[10,72,128]{2,1,0:T(8,128)S(1)} %get-tuple-element.94.unread), channel_id=1, source_target_pairs={{0,1},{1,2},{2,3},{3,4},{4,5},{5,6},{6,7},{7,0},{8,9},{9,10},{10,1... | collective-permute-start | bytes 1105928 | tf_op jit(solution)/shard_map/ppermute | solution.py:631
  46.6 4.8 %collective-permute-start.10 = (f32[16,128]{1,0:T(8,128)S(1)}, f32[16,128]{1,0:T(8,128)S(1)}, u32[]{:S(2)}, u32[]{:S(2)}) collective-permute-start(f32[16,128]{1,0:T(8,128)S(1)} %get-tuple-element.102), channel_id=1, source_target_pairs={{0,1},{1,0},{2,3},{3,2},{4,5},{5,4},{6,7},{7,6},{8,9},{9,8},{10,11... | collective-permute-start | bytes 24584 | tf_op jit(solution)/shard_map/ppermute | solution.py:678
  51.5 2.5 %collective-permute-start.11 = (f32[16,128]{1,0:T(8,128)S(1)}, f32[16,128]{1,0:T(8,128)S(1)}, u32[]{:S(2)}, u32[]{:S(2)}) collective-permute-start(f32[16,128]{1,0:T(8,128)S(1)} %add.38), channel_id=1, source_target_pairs={{0,2},{1,3},{2,0},{3,1},{4,6},{5,7},{6,4},{7,5},{8,10},{9,11},{10,... | collective-permute-start | bytes 24584 | tf_op jit(solution)/shard_map/ppermute | solution.py:678
  54.0 3.7 %collective-permute-start.12 = (f32[16,128]{1,0:T(8,128)S(1)}, f32[16,128]{1,0:T(8,128)S(1)}, u32[]{:S(2)}, u32[]{:S(2)}) collective-permute-start(f32[16,128]{1,0:T(8,128)S(1)} %add.39), channel_id=1, source_target_pairs={{0,6},{1,7},{2,4},{3,5},{4,2},{5,3},{6,0},{7,1},{8,14},{9,15},{10,... | collective-permute-start | bytes 24584 | tf_op jit(solution)/shard_map/ppermute | solution.py:678
  61.5 3.6 %collective-permute-start.13 = (f32[16,128]{1,0:T(8,128)S(1)}, f32[16,128]{1,0:T(8,128)S(1)}, u32[]{:S(2)}, u32[]{:S(2)}) collective-permute-start(f32[16,128]{1,0:T(8,128)S(1)} %get-tuple-element.122), channel_id=1, source_target_pairs={{0,1},{1,0},{2,3},{3,2},{4,5},{5,4},{6,7},{7,6},{8,9},{9,8},{10,11... | collective-permute-start | bytes 24584 | tf_op jit(solution)/shard_map/ppermute | solution.py:678
  65.1 2.5 %collective-permute-start.14 = (f32[16,128]{1,0:T(8,128)S(1)}, f32[16,128]{1,0:T(8,128)S(1)}, u32[]{:S(2)}, u32[]{:S(2)}) collective-permute-start(f32[16,128]{1,0:T(8,128)S(1)} %add.41), channel_id=1, source_target_pairs={{0,2},{1,3},{2,0},{3,1},{4,6},{5,7},{6,4},{7,5},{8,10},{9,11},{10,... | collective-permute-start | bytes 24584 | tf_op jit(solution)/shard_map/ppermute | solution.py:678
  67.6 3.7 %collective-permute-start.15 = (f32[16,128]{1,0:T(8,128)S(1)}, f32[16,128]{1,0:T(8,128)S(1)}, u32[]{:S(2)}, u32[]{:S(2)}) collective-permute-start(f32[16,128]{1,0:T(8,128)S(1)} %add.42), channel_id=1, source_target_pairs={{0,6},{1,7},{2,4},{3,5},{4,2},{5,3},{6,0},{7,1},{8,14},{9,15},{10,... | collective-permute-start | bytes 24584 | tf_op jit(solution)/shard_map/ppermute | solution.py:678
  95.8 2.9 %collective-permute-start.17 = (f32[10,8,128]{2,1,0:T(8,128)S(1)}, f32[10,8,128]{2,1,0:T(8,128)S(1)}, u32[]{:S(2)}, u32[]{:S(2)}) collective-permute-start(f32[10,8,128]{2,1,0:T(8,128)S(1)} %shard_map.89.near.moved), channel_id=1, source_target_pairs={{0,248},{8,0},{16,8},{24,16},{32,24},{40,32},{48,40},{56,48},{64,5... | collective-permute-start | bytes 122888 | tf_op jit(solution)/shard_map/ppermute | solution.py:631
  96.7 6.2 %collective-permute-start.16 = (f32[10,8,128]{2,1,0:T(8,128)S(1)}, f32[10,8,128]{2,1,0:T(8,128)S(1)}, u32[]{:S(2)}, u32[]{:S(2)}) collective-permute-start(f32[10,8,128]{2,1,0:T(8,128)S(1)} %shard_map.89.near.moved), channel_id=1, source_target_pairs={{0,8},{8,16},{16,24},{24,32},{32,40},{40,48},{48,56},{56,64},{64,7... | collective-permute-start | bytes 122888 | tf_op jit(solution)/shard_map/ppermute | solution.py:631
  103.0 3.1 %collective-permute-start.18 = (f32[5,24,128]{2,1,0:T(8,128)S(1)}, f32[5,24,128]{2,1,0:T(8,128)S(1)}, u32[]{:S(2)}, u32[]{:S(2)}) collective-permute-start(f32[5,24,128]{2,1,0:T(8,128)S(1)} %get-tuple-element.132), channel_id=1, source_target_pairs={{0,1},{1,2},{2,3},{3,4},{4,5},{5,6},{6,7},{7,0},{8,9},{9,10},{10,1... | collective-permute-start | bytes 184328 | tf_op jit(solution)/shard_map/ppermute | solution.py:631
  104.8 3.9 %collective-permute-start.19 = (f32[5,24,128]{2,1,0:T(8,128)S(1)}, f32[5,24,128]{2,1,0:T(8,128)S(1)}, u32[]{:S(2)}, u32[]{:S(2)}) collective-permute-start(f32[5,24,128]{2,1,0:T(8,128)S(1)} %get-tuple-element.133), channel_id=1, source_target_pairs={{0,7},{1,0},{2,1},{3,2},{4,3},{5,4},{6,5},{7,6},{8,15},{9,8},{10,9... | collective-permute-start | bytes 184328 | tf_op jit(solution)/shard_map/ppermute | solution.py:631
  108.8 7.6 %collective-permute-start.21 = (f32[20,24,128]{2,1,0:T(8,128)S(1)}, f32[20,24,128]{2,1,0:T(8,128)S(1)}, u32[]{:S(2)}, u32[]{:S(2)}) collective-permute-start(f32[20,24,128]{2,1,0:T(8,128)S(1)} %constant_dynamic-update-slice_fusion.refs_7_.refs_1_), channel_id=1, source_target_pairs={{0,232},{8,240},{16,248},{24,0},{32,8},{40,16},{48,24},{56,32},{64... | collective-permute-start | bytes 737288 | tf_op jit(solution)/shard_map/ppermute | solution.py:631
  108.8 8.8 %collective-permute-start.20 = (f32[20,24,128]{2,1,0:T(8,128)S(1)}, f32[20,24,128]{2,1,0:T(8,128)S(1)}, u32[]{:S(2)}, u32[]{:S(2)}) collective-permute-start(f32[20,24,128]{2,1,0:T(8,128)S(1)} %constant_dynamic-update-slice_fusion.refs_7_.refs_1_), channel_id=1, source_target_pairs={{0,24},{8,32},{16,40},{24,48},{32,56},{40,64},{48,72},{56,80},{64,... | collective-permute-start | bytes 737288 | tf_op jit(solution)/shard_map/ppermute | solution.py:631
  122.2 2.9 %collective-permute-start.22 = (f32[16,128]{1,0:T(8,128)S(1)}, f32[16,128]{1,0:T(8,128)S(1)}, u32[]{:S(2)}, u32[]{:S(2)}) collective-permute-start(f32[16,128]{1,0:T(8,128)S(1)} %get-tuple-element.148), channel_id=1, source_target_pairs={{0,1},{1,0},{2,3},{3,2},{4,5},{5,4},{6,7},{7,6},{8,9},{9,8},{10,11... | collective-permute-start | bytes 24584 | tf_op jit(solution)/shard_map/ppermute | solution.py:678
  125.1 2.5 %collective-permute-start.23 = (f32[16,128]{1,0:T(8,128)S(1)}, f32[16,128]{1,0:T(8,128)S(1)}, u32[]{:S(2)}, u32[]{:S(2)}) collective-permute-start(f32[16,128]{1,0:T(8,128)S(1)} %add.44), channel_id=1, source_target_pairs={{0,2},{1,3},{2,0},{3,1},{4,6},{5,7},{6,4},{7,5},{8,10},{9,11},{10,... | collective-permute-start | bytes 24584 | tf_op jit(solution)/shard_map/ppermute | solution.py:678
  127.6 3.7 %collective-permute-start.24 = (f32[16,128]{1,0:T(8,128)S(1)}, f32[16,128]{1,0:T(8,128)S(1)}, u32[]{:S(2)}, u32[]{:S(2)}) collective-permute-start(f32[16,128]{1,0:T(8,128)S(1)} %add.45), channel_id=1, source_target_pairs={{0,6},{1,7},{2,4},{3,5},{4,2},{5,3},{6,0},{7,1},{8,14},{9,15},{10,... | collective-permute-start | bytes 24584 | tf_op jit(solution)/shard_map/ppermute | solution.py:678
  135.5 3.6 %collective-permute-start.25 = (f32[16,128]{1,0:T(8,128)S(1)}, f32[16,128]{1,0:T(8,128)S(1)}, u32[]{:S(2)}, u32[]{:S(2)}) collective-permute-start(f32[16,128]{1,0:T(8,128)S(1)} %get-tuple-element.168), channel_id=1, source_target_pairs={{0,1},{1,0},{2,3},{3,2},{4,5},{5,4},{6,7},{7,6},{8,9},{9,8},{10,11... | collective-permute-start | bytes 24584 | tf_op jit(solution)/shard_map/ppermute | solution.py:678
  139.1 2.5 %collective-permute-start.26 = (f32[16,128]{1,0:T(8,128)S(1)}, f32[16,128]{1,0:T(8,128)S(1)}, u32[]{:S(2)}, u32[]{:S(2)}) collective-permute-start(f32[16,128]{1,0:T(8,128)S(1)} %add.47), channel_id=1, source_target_pairs={{0,2},{1,3},{2,0},{3,1},{4,6},{5,7},{6,4},{7,5},{8,10},{9,11},{10,... | collective-permute-start | bytes 24584 | tf_op jit(solution)/shard_map/ppermute | solution.py:678
  141.6 3.7 %collective-permute-start.27 = (f32[16,128]{1,0:T(8,128)S(1)}, f32[16,128]{1,0:T(8,128)S(1)}, u32[]{:S(2)}, u32[]{:S(2)}) collective-permute-start(f32[16,128]{1,0:T(8,128)S(1)} %add.48), channel_id=1, source_target_pairs={{0,6},{1,7},{2,4},{3,5},{4,2},{5,3},{6,0},{7,1},{8,14},{9,15},{10,... | collective-permute-start | bytes 24584 | tf_op jit(solution)/shard_map/ppermute | solution.py:678
  145.3 25.0 %copy-start = (f32[10,8,128]{2,1,0:T(8,128)S(1)}, f32[10,8,128]{2,1,0:T(8,128)}, u32[]{:S(2)}) copy-start(f32[10,8,128]{2,1,0:T(8,128)} %head.1) | copy-start | bytes 122884
where the time goes:
time: 172 us
  waiting for transfers between devices  52.6 us (31%)
  blocking collectives  44.1 us (26%)
  starting transfers between devices  40.5 us (24%)
  Pallas kernels  33.1 us (19%)
    all_to_all x2, blocking collectives, summed_over_all(): lax.all_to_all(jnp.broadcast_to(row[None], (count, 1, 128)), axes, 0, 0,...  44.1 us
    pallas_call x14, Pallas kernels, call(): pl.pallas_call(kernel, out_shape=outs, in_specs=place, out_specs=spec, sc...  33.1 us
    ppermute x16, waiting for transfers between devices, shifted(): lax.ppermute(field, axis, [(i, (i + by) % count) for i in range(count)])  26.7 us
    ppermute x16, starting transfers between devices, shifted(): lax.ppermute(field, axis, [(i, (i + by) % count) for i in range(count)])  26.7 us
    ppermute x12, waiting for transfers between devices, summed(): lax.ppermute(field, 'gy', [(i, i ^ flip) for i in range(count)])  25.9 us
    ppermute x12, starting transfers between devices, summed(): lax.ppermute(field, 'gy', [(i, i ^ flip) for i in range(count)])  13.8 us
  transfers between devices with their start and end apart: 28, of which 26 were waited for; matrix products, arithmetic and copies ran while one was open for 0% of the time, Pallas kernels for 4%

commit v1 on v0

--- a/solution.py
+++ b/solution.py
@@ -702,8 +702,10 @@
         range(4),
     )
     near = jnp.concatenate([shifted(start, "gx", 1), start, shifted(start, "gx", -1)], axis=1)
-    soil_cells = sideways(packed(wider(near[:NZ])))
-    packs = packed(wider(near[NZ:]), soil_cells[1:])
+    parts = wider(near)
+    soil_packs = packed([part[:NZ] for part in parts])
+    soil_cells = sideways(soil_packs)
+    packs = packed([part[NZ:] for part in parts], soil_packs[1:])
     cells = sideways(packs)
     given = soil_fields([tables, *soil_cells, packs[1]])
     moved = None

time: 172 us -> 172 us (level)
  waiting for transfers between devices: 52.6 us -> 57 us
  starting transfers between devices: 40.5 us -> 36.6 us
    ppermute x16 -> x14, waiting for transfers between devices: 26.7 us -> 33.8 us  [shifted(): lax.ppermute(field, axis, [(i, (i + by) % count) for i in range(count)])]
    ppermute x16 -> x14, starting transfers between devices: 26.7 us -> 22.3 us  [shifted(): lax.ppermute(field, axis, [(i, (i + by) % count) for i in range(count)])]
    ppermute x12, waiting for transfers between devices: 25.9 us -> 23.2 us  [summed(): lax.ppermute(field, 'gy', [(i, i ^ flip) for i in range(count)])]
  transfers between devices with their start and end apart: 28 -> 26, of which waited for: 26 -> 24; matrix products, arithmetic and copies ran while one was open for 0% -> 0% of each run, Pallas kernels for 4% -> 4%
where the time goes in v1:
time: 172 us
  waiting for transfers between devices  57 us (33%)
  blocking collectives  43.8 us (25%)
  starting transfers between devices  36.6 us (21%)
  Pallas kernels  33.1 us (19%)
    all_to_all x2, blocking collectives, summed_over_all(): lax.all_to_all(jnp.broadcast_to(row[None], (count, 1, 128)), axes, 0, 0,...  43.8 us
    ppermute x14, waiting for transfers between devices, shifted(): lax.ppermute(field, axis, [(i, (i + by) % count) for i in range(count)])  33.8 us
    pallas_call x14, Pallas kernels, call(): pl.pallas_call(kernel, out_shape=outs, in_specs=place, out_specs=spec, sc...  33.1 us
    ppermute x12, waiting for transfers between devices, summed(): lax.ppermute(field, 'gy', [(i, i ^ flip) for i in range(count)])  23.2 us
    ppermute x14, starting transfers between devices, shifted(): lax.ppermute(field, axis, [(i, (i + by) % count) for i in range(count)])  22.3 us
    ppermute x12, starting transfers between devices, summed(): lax.ppermute(field, 'gy', [(i, i ^ flip) for i in range(count)])  14.3 us
  transfers between devices with their start and end apart: 26, of which 24 were waited for; matrix products, arithmetic and copies ran while one was open for 0% of the time, Pallas kernels for 4%

profile of v1, /device:TPU:1, one launch (start us, length us, event | category | flops | bytes accessed | tf_op | source)
XLA Modules:
  0.0 171.9 jit_solution(7686597054126748123)
XLA Ops:
  2.1 8.7 %collective-permute-start.1 = (f32[30,8,128]{2,1,0:T(8,128)S(1)}, f32[30,8,128]{2,1,0:T(8,128)S(1)}, u32[]{:S(2)}, u32[]{:S(2)}) collective-permute-start(f32[30,8,128]{2,1,0:T(8,128)S(1)} %shard_map.82), channel_id=1, source_target_pairs={{0,248},{8,0},{16,8},{24,16},{32,24},{40,32},{48,40},{56,48},{64,5... | collective-permute-start | bytes 368648 | tf_op jit(solution)/shard_map/ppermute | solution.py:631
  10.7 1.9 %collective-permute-done.1 = f32[30,8,128]{2,1,0:T(8,128)S(1)} collective-permute-done((f32[30,8,128]{2,1,0:T(8,128)S(1)}, f32[30,8,128]{2,1,0:T(8,128)S(1)}, u32[]{:S(2)}, u32[]{:S(2)}) %collective-permute-start.1) | collective-permute-done | bytes 122912 | tf_op jit(solution)/shard_map/ppermute | solution.py:631
  12.6 5.2 %collective-permute-done = f32[30,8,128]{2,1,0:T(8,128)S(1)} collective-permute-done((f32[30,8,128]{2,1,0:T(8,128)S(1)}, f32[30,8,128]{2,1,0:T(8,128)S(1)}, u32[]{:S(2)}, u32[]{:S(2)}) %collective-permute-start) | collective-permute-done | bytes 122912 | tf_op jit(solution)/shard_map/ppermute | solution.py:631
  17.9 2.7 %collective-permute-start.2 = (f32[30,24,128]{2,1,0:T(8,128)S(1)}, f32[30,24,128]{2,1,0:T(8,128)S(1)}, u32[]{:S(2)}, u32[]{:S(2)}) collective-permute-start(f32[30,24,128]{2,1,0:T(8,128)S(1)} %pad_maximum_fusion), channel_id=1, source_target_pairs={{0,24},{8,32},{16,40},{24,48},{32,56},{40,64},{48,72},{56,80},{64,... | collective-permute-start | bytes 1105928 | tf_op jit(solution)/shard_map/ppermute | solution.py:631
  20.6 6.5 %collective-permute-done.3 = f32[30,24,128]{2,1,0:T(8,128)S(1)} collective-permute-done((f32[30,24,128]{2,1,0:T(8,128)S(1)}, f32[30,24,128]{2,1,0:T(8,128)S(1)}, u32[]{:S(2)}, u32[]{:S(2)}) %collective-permute-start.3) | collective-permute-done | bytes 368672 | tf_op jit(solution)/shard_map/ppermute | solution.py:631
  28.9 3.0 %collective-permute-start.5 = (f32[10,72,128]{2,1,0:T(8,128)S(1)}, f32[10,72,128]{2,1,0:T(8,128)S(1)}, u32[]{:S(2)}, u32[]{:S(2)}) collective-permute-start(f32[10,72,128]{2,1,0:T(8,128)S(1)} %get-tuple-element.95), channel_id=1, source_target_pairs={{0,7},{1,0},{2,1},{3,2},{4,3},{5,4},{6,5},{7,6},{8,15},{9,8},{10,9... | collective-permute-start | bytes 1105928 | tf_op jit(solution)/shard_map/ppermute | solution.py:631
  33.7 5.9 %collective-permute-done.6.left = f32[5,72,128]{2,1,0:T(8,128)S(1)} collective-permute-done((f32[5,72,128]{2,1,0:T(8,128)S(1)}, f32[5,72,128]{2,1,0:T(8,128)S(1)}, u32[]{:S(2)}, u32[]{:S(2)}) %collective-permute-start.6) | collective-permute-done | bytes 184352 | tf_op jit(solution)/shard_map/ppermute | solution.py:631
  40.6 3.6 %shard_map.85 = (f32[10,8,24,128]{3,2,1,0:T(8,128)S(1)}, f32[10,8,24,128]{3,2,1,0:T(8,128)S(1)}, f32[10,8,24,128]{3,2,1,0:T(8,128)S(1)}, f32[10,8,24,128]{3,2,1,0:T(8,128)S(1)}, f32[10,8,24,128]{3,2,1,0:T(8,128)S(1)}) custom-call(f32[4,8,128]{2,1,0:T(8,128)S(1)} %broadcast_in_dim.10.tables, f32[10,72,128]{2,1,0:T(8,128)S(1)} %get-tuple-element.96.cells, ...), custom_call_target="tpu_custom_call" | custom-call | flops 10000000 | bytes 20000000 | tf_op jit(solution)/shard_map/pallas_call | solution.py:582
  44.3 5.3 %shard_map.86 = (f32[10,8,24,128]{3,2,1,0:T(8,128)S(1)}, f32[10,8,24,128]{3,2,1,0:T(8,128)S(1)}, f32[10,8,24,128]{3,2,1,0:T(8,128)S(1)}, f32[11,8,24,128]{3,2,1,...) custom-call(f32[20,72,128]{2,1,0:T(8,128)S(1)} %get-tuple-element.93, ...), custom_call_target="tpu_custom_call" | custom-call | tf_op jit(solution)/shard_map/pallas_call | solution.py:582
  52.1 2.5 %collective-permute-done.9 = f32[16,128]{1,0:T(8,128)S(1)} collective-permute-done((f32[16,128]{1,0:T(8,128)S(1)}, f32[16,128]{1,0:T(8,128)S(1)}, u32[]{:S(2)}, u32[]{:S(2)}) %collective-permute-start.9) | collective-permute-done | bytes 8224 | tf_op jit(solution)/shard_map/ppermute | solution.py:678
  56.0 2.3 %collective-permute-done.10 = f32[16,128]{1,0:T(8,128)S(1)} collective-permute-done((f32[16,128]{1,0:T(8,128)S(1)}, f32[16,128]{1,0:T(8,128)S(1)}, u32[]{:S(2)}, u32[]{:S(2)}) %collective-permute-start.10) | collective-permute-done | bytes 8224 | tf_op jit(solution)/shard_map/ppermute | solution.py:678
  58.4 3.9 %shard_map.87 = (f32[10,8,16,128]{3,2,1,0:T(8,128)S(1)}, f32[10,8,16,128]{3,2,1,0:T(8,128)S(1)}, f32[10,2,16,128]{3,2,1,0:T(8,128)S(1)}, f32[10,2,16,128]{3,2,1,...) custom-call(f32[16,128]{1,0:T(8,128)S(1)} %add.40.total.weight, ...), custom_call_target="tpu_custom_call" | custom-call | tf_op jit(solution)/shard_map/pallas_call | solution.py:582
  62.2 2.7 %collective-permute-start.11 = (f32[16,128]{1,0:T(8,128)S(1)}, f32[16,128]{1,0:T(8,128)S(1)}, u32[]{:S(2)}, u32[]{:S(2)}) collective-permute-start(f32[16,128]{1,0:T(8,128)S(1)} %get-tuple-element.122), channel_id=1, source_target_pairs={{0,1},{1,0},{2,3},{3,2},{4,5},{5,4},{6,7},{7,6},{8,9},{9,8},{10,11... | collective-permute-start | bytes 24584 | tf_op jit(solution)/shard_map/ppermute | solution.py:678
  65.8 2.5 %collective-permute-done.12 = f32[16,128]{1,0:T(8,128)S(1)} collective-permute-done((f32[16,128]{1,0:T(8,128)S(1)}, f32[16,128]{1,0:T(8,128)S(1)}, u32[]{:S(2)}, u32[]{:S(2)}) %collective-permute-start.12) | collective-permute-done | bytes 8224 | tf_op jit(solution)/shard_map/ppermute | solution.py:678
  69.7 2.3 %collective-permute-done.13 = f32[16,128]{1,0:T(8,128)S(1)} collective-permute-done((f32[16,128]{1,0:T(8,128)S(1)}, f32[16,128]{1,0:T(8,128)S(1)}, u32[]{:S(2)}, u32[]{:S(2)}) %collective-permute-start.13) | collective-permute-done | bytes 8224 | tf_op jit(solution)/shard_map/ppermute | solution.py:678
  72.0 2.2 %shard_map.88 = (f32[1,128]{1,0:T(1,128)S(1)}, f32[10,8,128]{2,1,0:T(8,128)S(1)}) custom-call(f32[16,128]{1,0:T(8,128)S(1)} %add.43.total, f32[16,128]{1,0:T(8,128)S(1)} %add.40.total.weight, f32[10,8,24,128]{3,2,1,0:T(8,128)S(1)} %get-tuple-element.103.c0, f32[10,8,24,128]{3,2,1,0:T(8,128)S(1)} %get-tuple-element.104.w0, ...), custom_call_target="tpu_custom_call" | custom-call | tf_op jit(solution)/shard_map/pallas_call | solution.py:582
  74.3 21.3 %all_to_all.10 = f32[256,1,128]{2,1,0:T(1,128)S(1)} all-to-all(f32[256,1,128]{2,1,0:T(1,128)S(1)} %broadcast_in_dim.24), channel_id=1, replica_groups=mesh['gx'=32,'gy'=8] {'gx','gy'}, dimensions={0} | all-to-all | bytes 262144 | tf_op jit(solution)/shard_map/all_to_all | solution.py:685
  99.0 4.2 %collective-permute-done.14.west = f32[10,8,128]{2,1,0:T(8,128)S(1)} collective-permute-done((f32[10,8,128]{2,1,0:T(8,128)S(1)}, f32[10,8,128]{2,1,0:T(8,128)S(1)}, u32[]{:S(2)}, u32[]{:S(2)}) %collective-permute-start.14) | collective-permute-done | bytes 40992 | tf_op jit(solution)/shard_map/ppermute | solution.py:631
  103.3 1.8 %collective-permute-start.16 = (f32[5,24,128]{2,1,0:T(8,128)S(1)}, f32[5,24,128]{2,1,0:T(8,128)S(1)}, u32[]{:S(2)}, u32[]{:S(2)}) collective-permute-start(f32[5,24,128]{2,1,0:T(8,128)S(1)} %get-tuple-element.132), channel_id=1, source_target_pairs={{0,1},{1,2},{2,3},{3,4},{4,5},{5,6},{6,7},{7,0},{8,9},{9,10},{10,1... | collective-permute-start | bytes 184328 | tf_op jit(solution)/shard_map/ppermute | solution.py:631
  106.4 2.6 %collective-permute-done.17 = f32[5,24,128]{2,1,0:T(8,128)S(1)} collective-permute-done((f32[5,24,128]{2,1,0:T(8,128)S(1)}, f32[5,24,128]{2,1,0:T(8,128)S(1)}, u32[]{:S(2)}, u32[]{:S(2)}) %collective-permute-start.17) | collective-permute-done | bytes 61472 | tf_op jit(solution)/shard_map/ppermute | solution.py:631
  109.1 2.7 %collective-permute-start.18 = (f32[20,24,128]{2,1,0:T(8,128)S(1)}, f32[20,24,128]{2,1,0:T(8,128)S(1)}, u32[]{:S(2)}, u32[]{:S(2)}) collective-permute-start(f32[20,24,128]{2,1,0:T(8,128)S(1)} %constant_dynamic-update-slice_fusion.refs_7_.refs_1_), channel_id=1, source_target_pairs={{0,24},{8,32},{16,40},{24,48},{32,56},{40,64},{48,72},{56,80},{64,... | collective-permute-start | bytes 737288 | tf_op jit(solution)/shard_map/ppermute | solution.py:631
  111.8 3.0 %shard_map.91 = (f32[10,8,24,128]{3,2,1,0:T(8,128)S(1)}, f32[10,8,24,128]{3,2,1,0:T(8,128)S(1)}, f32[10,8,24,128]{3,2,1,0:T(8,128)S(1)}, f32[10,8,24,128]{3,2,1,...) custom-call(f32[10,8,24,128]{3,2,1,0:T(8,128)} %get-tuple-element.134, ...), custom_call_target="tpu_custom_call" | custom-call | flops 1000000 | bytes 15000000 | tf_op jit(solution)/shard_map/pallas_call | solution.py:582
  117.8 4.7 %shard_map.92 = (f32[10,8,24,128]{3,2,1,0:T(8,128)S(1)}, f32[10,8,24,128]{3,2,1,0:T(8,128)S(1)}, f32[10,8,24,128]{3,2,1,0:T(8,128)S(1)}, f32[11,8,24,128]{3,2,1,...) custom-call(f32[20,24,128]{2,1,0:T(8,128)S(1)} %collective-permute-d, ...), custom_call_target="tpu_custom_call" | custom-call | tf_op jit(solution)/shard_map/pallas_call | solution.py:582
  122.5 2.1 %collective-permute-start.20 = (f32[16,128]{1,0:T(8,128)S(1)}, f32[16,128]{1,0:T(8,128)S(1)}, u32[]{:S(2)}, u32[]{:S(2)}) collective-permute-start(f32[16,128]{1,0:T(8,128)S(1)} %get-tuple-element.148), channel_id=1, source_target_pairs={{0,1},{1,0},{2,3},{3,2},{4,5},{5,4},{6,7},{7,6},{8,9},{9,8},{10,11... | collective-permute-start | bytes 24584 | tf_op jit(solution)/shard_map/ppermute | solution.py:678
  125.5 2.5 %collective-permute-done.21 = f32[16,128]{1,0:T(8,128)S(1)} collective-permute-done((f32[16,128]{1,0:T(8,128)S(1)}, f32[16,128]{1,0:T(8,128)S(1)}, u32[]{:S(2)}, u32[]{:S(2)}) %collective-permute-start.21) | collective-permute-done | bytes 8224 | tf_op jit(solution)/shard_map/ppermute | solution.py:678
  129.2 2.5 %collective-permute-done.22 = f32[16,128]{1,0:T(8,128)S(1)} collective-permute-done((f32[16,128]{1,0:T(8,128)S(1)}, f32[16,128]{1,0:T(8,128)S(1)}, u32[]{:S(2)}, u32[]{:S(2)}) %collective-permute-start.22) | collective-permute-done | bytes 8224 | tf_op jit(solution)/shard_map/ppermute | solution.py:678
  131.7 4.1 %shard_map.93 = (f32[10,8,16,128]{3,2,1,0:T(8,128)S(1)}, f32[10,8,16,128]{3,2,1,0:T(8,128)S(1)}, f32[10,2,16,128]{3,2,1,0:T(8,128)S(1)}, f32[10,2,16,128]{3,2,1,...) custom-call(f32[16,128]{1,0:T(8,128)S(1)} %add.46.total.weight, ...), custom_call_target="tpu_custom_call" | custom-call | tf_op jit(solution)/shard_map/pallas_call | solution.py:582
  135.8 2.7 %collective-permute-start.23 = (f32[16,128]{1,0:T(8,128)S(1)}, f32[16,128]{1,0:T(8,128)S(1)}, u32[]{:S(2)}, u32[]{:S(2)}) collective-permute-start(f32[16,128]{1,0:T(8,128)S(1)} %get-tuple-element.168), channel_id=1, source_target_pairs={{0,1},{1,0},{2,3},{3,2},{4,5},{5,4},{6,7},{7,6},{8,9},{9,8},{10,11... | collective-permute-start | bytes 24584 | tf_op jit(solution)/shard_map/ppermute | solution.py:678
  139.4 2.5 %collective-permute-done.24 = f32[16,128]{1,0:T(8,128)S(1)} collective-permute-done((f32[16,128]{1,0:T(8,128)S(1)}, f32[16,128]{1,0:T(8,128)S(1)}, u32[]{:S(2)}, u32[]{:S(2)}) %collective-permute-start.24) | collective-permute-done | bytes 8224 | tf_op jit(solution)/shard_map/ppermute | solution.py:678
  142.9 2.7 %collective-permute-done.25 = f32[16,128]{1,0:T(8,128)S(1)} collective-permute-done((f32[16,128]{1,0:T(8,128)S(1)}, f32[16,128]{1,0:T(8,128)S(1)}, u32[]{:S(2)}, u32[]{:S(2)}) %collective-permute-start.25) | collective-permute-done | bytes 8224 | tf_op jit(solution)/shard_map/ppermute | solution.py:678
  145.6 2.4 %shard_map.94 = (f32[1,128]{1,0:T(1,128)S(1)}, f32[10,8,128]{2,1,0:T(8,128)S(1)}) custom-call(f32[16,128]{1,0:T(8,128)S(1)} %add.49.total, f32[16,128]{1,0:T(8,128)S(1)} %add.46.total.weight, f32[10,8,24,128]{3,2,1,0:T(8,128)S(1)} %get-tuple-element.149.c0, f32[10,8,24,128]{3,2,1,0:T(8,128)S(1)} %get-tuple-element.150.w0, ...), custom_call_target="tpu_custom_call" | custom-call | tf_op jit(solution)/shard_map/pallas_call | solution.py:582
  148.1 22.5 %all_to_all.11 = f32[256,1,128]{2,1,0:T(1,128)S(1)} all-to-all(f32[256,1,128]{2,1,0:T(1,128)S(1)} %broadcast_in_dim.26), channel_id=1, replica_groups=mesh['gx'=32,'gy'=8] {'gx','gy'}, dimensions={0} | all-to-all | bytes 262144 | tf_op jit(solution)/shard_map/all_to_all | solution.py:685
  (66 shorter events, 26.1 us)
Async XLA Ops:
  2.1 10.6 %collective-permute-start.1 = (f32[30,8,128]{2,1,0:T(8,128)S(1)}, f32[30,8,128]{2,1,0:T(8,128)S(1)}, u32[]{:S(2)}, u32[]{:S(2)}) collective-permute-start(f32[30,8,128]{2,1,0:T(8,128)S(1)} %shard_map.82), channel_id=1, source_target_pairs={{0,248},{8,0},{16,8},{24,16},{32,24},{40,32},{48,40},{56,48},{64,5... | collective-permute-start | bytes 368648 | tf_op jit(solution)/shard_map/ppermute | solution.py:631
  10.7 7.1 %collective-permute-start = (f32[30,8,128]{2,1,0:T(8,128)S(1)}, f32[30,8,128]{2,1,0:T(8,128)S(1)}, u32[]{:S(2)}, u32[]{:S(2)}) collective-permute-start(f32[30,8,128]{2,1,0:T(8,128)S(1)} %shard_map.82), channel_id=1, source_target_pairs={{0,8},{8,16},{16,24},{24,32},{32,40},{40,48},{48,56},{56,64},{64,7... | collective-permute-start | bytes 368648 | tf_op jit(solution)/shard_map/ppermute | solution.py:631
  17.8 9.3 %collective-permute-start.3 = (f32[30,24,128]{2,1,0:T(8,128)S(1)}, f32[30,24,128]{2,1,0:T(8,128)S(1)}, u32[]{:S(2)}, u32[]{:S(2)}) collective-permute-start(f32[30,24,128]{2,1,0:T(8,128)S(1)} %pad_maximum_fusion), channel_id=1, source_target_pairs={{0,232},{8,240},{16,248},{24,0},{32,8},{40,16},{48,24},{56,32},{64... | collective-permute-start | bytes 1105928 | tf_op jit(solution)/shard_map/ppermute | solution.py:631
  17.9 10.2 %collective-permute-start.2 = (f32[30,24,128]{2,1,0:T(8,128)S(1)}, f32[30,24,128]{2,1,0:T(8,128)S(1)}, u32[]{:S(2)}, u32[]{:S(2)}) collective-permute-start(f32[30,24,128]{2,1,0:T(8,128)S(1)} %pad_maximum_fusion), channel_id=1, source_target_pairs={{0,24},{8,32},{16,40},{24,48},{32,56},{40,64},{48,72},{56,80},{64,... | collective-permute-start | bytes 1105928 | tf_op jit(solution)/shard_map/ppermute | solution.py:631
  28.9 15.3 %collective-permute-start.5 = (f32[10,72,128]{2,1,0:T(8,128)S(1)}, f32[10,72,128]{2,1,0:T(8,128)S(1)}, u32[]{:S(2)}, u32[]{:S(2)}) collective-permute-start(f32[10,72,128]{2,1,0:T(8,128)S(1)} %get-tuple-element.95), channel_id=1, source_target_pairs={{0,7},{1,0},{2,1},{3,2},{4,3},{5,4},{6,5},{7,6},{8,15},{9,8},{10,9... | collective-permute-start | bytes 1105928 | tf_op jit(solution)/shard_map/ppermute | solution.py:631
  32.0 12.3 %collective-permute-start.4 = (f32[10,72,128]{2,1,0:T(8,128)S(1)}, f32[10,72,128]{2,1,0:T(8,128)S(1)}, u32[]{:S(2)}, u32[]{:S(2)}) collective-permute-start(f32[10,72,128]{2,1,0:T(8,128)S(1)} %get-tuple-element.94.unread), channel_id=1, source_target_pairs={{0,1},{1,2},{2,3},{3,4},{4,5},{5,6},{6,7},{7,0},{8,9},{9,10},{10,1... | collective-permute-start | bytes 1105928 | tf_op jit(solution)/shard_map/ppermute | solution.py:631
  33.2 6.4 %collective-permute-start.6 = (f32[5,72,128]{2,1,0:T(8,128)S(1)}, f32[5,72,128]{2,1,0:T(8,128)S(1)}, u32[]{:S(2)}, u32[]{:S(2)}) collective-permute-start(f32[5,72,128]{2,1,0:T(8,128)S(1)} %get-tuple-element.91.refs_0_), channel_id=1, source_target_pairs={{0,1},{1,2},{2,3},{3,4},{4,5},{5,6},{6,7},{7,0},{8,9},{9,10},{10,1... | collective-permute-start | bytes 552968 | tf_op jit(solution)/shard_map/ppermute | solution.py:631
  33.7 7.0 %collective-permute-start.7 = (f32[5,72,128]{2,1,0:T(8,128)S(1)}, f32[5,72,128]{2,1,0:T(8,128)S(1)}, u32[]{:S(2)}, u32[]{:S(2)}) collective-permute-start(f32[5,72,128]{2,1,0:T(8,128)S(1)} %get-tuple-element.92.refs_1_), channel_id=1, source_target_pairs={{0,7},{1,0},{2,1},{3,2},{4,3},{5,4},{6,5},{7,6},{8,15},{9,8},{10,9... | collective-permute-start | bytes 552968 | tf_op jit(solution)/shard_map/ppermute | solution.py:631
  49.6 2.6 %collective-permute-start.8 = (f32[16,128]{1,0:T(8,128)S(1)}, f32[16,128]{1,0:T(8,128)S(1)}, u32[]{:S(2)}, u32[]{:S(2)}) collective-permute-start(f32[16,128]{1,0:T(8,128)S(1)} %get-tuple-element.102), channel_id=1, source_target_pairs={{0,1},{1,0},{2,3},{3,2},{4,5},{5,4},{6,7},{7,6},{8,9},{9,8},{10,11... | collective-permute-start | bytes 24584 | tf_op jit(solution)/shard_map/ppermute | solution.py:678
  52.1 2.5 %collective-permute-start.9 = (f32[16,128]{1,0:T(8,128)S(1)}, f32[16,128]{1,0:T(8,128)S(1)}, u32[]{:S(2)}, u32[]{:S(2)}) collective-permute-start(f32[16,128]{1,0:T(8,128)S(1)} %add.38), channel_id=1, source_target_pairs={{0,2},{1,3},{2,0},{3,1},{4,6},{5,7},{6,4},{7,5},{8,10},{9,11},{10,... | collective-permute-start | bytes 24584 | tf_op jit(solution)/shard_map/ppermute | solution.py:678
  54.6 3.7 %collective-permute-start.10 = (f32[16,128]{1,0:T(8,128)S(1)}, f32[16,128]{1,0:T(8,128)S(1)}, u32[]{:S(2)}, u32[]{:S(2)}) collective-permute-start(f32[16,128]{1,0:T(8,128)S(1)} %add.39), channel_id=1, source_target_pairs={{0,6},{1,7},{2,4},{3,5},{4,2},{5,3},{6,0},{7,1},{8,14},{9,15},{10,... | collective-permute-start | bytes 24584 | tf_op jit(solution)/shard_map/ppermute | solution.py:678
  62.2 3.6 %collective-permute-start.11 = (f32[16,128]{1,0:T(8,128)S(1)}, f32[16,128]{1,0:T(8,128)S(1)}, u32[]{:S(2)}, u32[]{:S(2)}) collective-permute-start(f32[16,128]{1,0:T(8,128)S(1)} %get-tuple-element.122), channel_id=1, source_target_pairs={{0,1},{1,0},{2,3},{3,2},{4,5},{5,4},{6,7},{7,6},{8,9},{9,8},{10,11... | collective-permute-start | bytes 24584 | tf_op jit(solution)/shard_map/ppermute | solution.py:678
  65.8 2.5 %collective-permute-start.12 = (f32[16,128]{1,0:T(8,128)S(1)}, f32[16,128]{1,0:T(8,128)S(1)}, u32[]{:S(2)}, u32[]{:S(2)}) collective-permute-start(f32[16,128]{1,0:T(8,128)S(1)} %add.41), channel_id=1, source_target_pairs={{0,2},{1,3},{2,0},{3,1},{4,6},{5,7},{6,4},{7,5},{8,10},{9,11},{10,... | collective-permute-start | bytes 24584 | tf_op jit(solution)/shard_map/ppermute | solution.py:678
  68.3 3.7 %collective-permute-start.13 = (f32[16,128]{1,0:T(8,128)S(1)}, f32[16,128]{1,0:T(8,128)S(1)}, u32[]{:S(2)}, u32[]{:S(2)}) collective-permute-start(f32[16,128]{1,0:T(8,128)S(1)} %add.42), channel_id=1, source_target_pairs={{0,6},{1,7},{2,4},{3,5},{4,2},{5,3},{6,0},{7,1},{8,14},{9,15},{10,... | collective-permute-start | bytes 24584 | tf_op jit(solution)/shard_map/ppermute | solution.py:678
  96.1 2.9 %collective-permute-start.15 = (f32[10,8,128]{2,1,0:T(8,128)S(1)}, f32[10,8,128]{2,1,0:T(8,128)S(1)}, u32[]{:S(2)}, u32[]{:S(2)}) collective-permute-start(f32[10,8,128]{2,1,0:T(8,128)S(1)} %shard_map.89.near.moved), channel_id=1, source_target_pairs={{0,248},{8,0},{16,8},{24,16},{32,24},{40,32},{48,40},{56,48},{64,5... | collective-permute-start | bytes 122888 | tf_op jit(solution)/shard_map/ppermute | solution.py:631
  97.0 6.2 %collective-permute-start.14 = (f32[10,8,128]{2,1,0:T(8,128)S(1)}, f32[10,8,128]{2,1,0:T(8,128)S(1)}, u32[]{:S(2)}, u32[]{:S(2)}) collective-permute-start(f32[10,8,128]{2,1,0:T(8,128)S(1)} %shard_map.89.near.moved), channel_id=1, source_target_pairs={{0,8},{8,16},{16,24},{24,32},{32,40},{40,48},{48,56},{56,64},{64,7... | collective-permute-start | bytes 122888 | tf_op jit(solution)/shard_map/ppermute | solution.py:631
  103.3 3.1 %collective-permute-start.16 = (f32[5,24,128]{2,1,0:T(8,128)S(1)}, f32[5,24,128]{2,1,0:T(8,128)S(1)}, u32[]{:S(2)}, u32[]{:S(2)}) collective-permute-start(f32[5,24,128]{2,1,0:T(8,128)S(1)} %get-tuple-element.132), channel_id=1, source_target_pairs={{0,1},{1,2},{2,3},{3,4},{4,5},{5,6},{6,7},{7,0},{8,9},{9,10},{10,1... | collective-permute-start | bytes 184328 | tf_op jit(solution)/shard_map/ppermute | solution.py:631
  105.1 3.9 %collective-permute-start.17 = (f32[5,24,128]{2,1,0:T(8,128)S(1)}, f32[5,24,128]{2,1,0:T(8,128)S(1)}, u32[]{:S(2)}, u32[]{:S(2)}) collective-permute-start(f32[5,24,128]{2,1,0:T(8,128)S(1)} %get-tuple-element.133), channel_id=1, source_target_pairs={{0,7},{1,0},{2,1},{3,2},{4,3},{5,4},{6,5},{7,6},{8,15},{9,8},{10,9... | collective-permute-start | bytes 184328 | tf_op jit(solution)/shard_map/ppermute | solution.py:631
  109.1 7.6 %collective-permute-start.19 = (f32[20,24,128]{2,1,0:T(8,128)S(1)}, f32[20,24,128]{2,1,0:T(8,128)S(1)}, u32[]{:S(2)}, u32[]{:S(2)}) collective-permute-start(f32[20,24,128]{2,1,0:T(8,128)S(1)} %constant_dynamic-update-slice_fusion.refs_7_.refs_1_), channel_id=1, source_target_pairs={{0,232},{8,240},{16,248},{24,0},{32,8},{40,16},{48,24},{56,32},{64... | collective-permute-start | bytes 737288 | tf_op jit(solution)/shard_map/ppermute | solution.py:631
  109.1 8.8 %collective-permute-start.18 = (f32[20,24,128]{2,1,0:T(8,128)S(1)}, f32[20,24,128]{2,1,0:T(8,128)S(1)}, u32[]{:S(2)}, u32[]{:S(2)}) collective-permute-start(f32[20,24,128]{2,1,0:T(8,128)S(1)} %constant_dynamic-update-slice_fusion.refs_7_.refs_1_), channel_id=1, source_target_pairs={{0,24},{8,32},{16,40},{24,48},{32,56},{40,64},{48,72},{56,80},{64,... | collective-permute-start | bytes 737288 | tf_op jit(solution)/shard_map/ppermute | solution.py:631
  122.5 2.9 %collective-permute-start.20 = (f32[16,128]{1,0:T(8,128)S(1)}, f32[16,128]{1,0:T(8,128)S(1)}, u32[]{:S(2)}, u32[]{:S(2)}) collective-permute-start(f32[16,128]{1,0:T(8,128)S(1)} %get-tuple-element.148), channel_id=1, source_target_pairs={{0,1},{1,0},{2,3},{3,2},{4,5},{5,4},{6,7},{7,6},{8,9},{9,8},{10,11... | collective-permute-start | bytes 24584 | tf_op jit(solution)/shard_map/ppermute | solution.py:678
  125.5 2.5 %collective-permute-start.21 = (f32[16,128]{1,0:T(8,128)S(1)}, f32[16,128]{1,0:T(8,128)S(1)}, u32[]{:S(2)}, u32[]{:S(2)}) collective-permute-start(f32[16,128]{1,0:T(8,128)S(1)} %add.44), channel_id=1, source_target_pairs={{0,2},{1,3},{2,0},{3,1},{4,6},{5,7},{6,4},{7,5},{8,10},{9,11},{10,... | collective-permute-start | bytes 24584 | tf_op jit(solution)/shard_map/ppermute | solution.py:678
  128.0 3.7 %collective-permute-start.22 = (f32[16,128]{1,0:T(8,128)S(1)}, f32[16,128]{1,0:T(8,128)S(1)}, u32[]{:S(2)}, u32[]{:S(2)}) collective-permute-start(f32[16,128]{1,0:T(8,128)S(1)} %add.45), channel_id=1, source_target_pairs={{0,6},{1,7},{2,4},{3,5},{4,2},{5,3},{6,0},{7,1},{8,14},{9,15},{10,... | collective-permute-start | bytes 24584 | tf_op jit(solution)/shard_map/ppermute | solution.py:678
  135.8 3.6 %collective-permute-start.23 = (f32[16,128]{1,0:T(8,128)S(1)}, f32[16,128]{1,0:T(8,128)S(1)}, u32[]{:S(2)}, u32[]{:S(2)}) collective-permute-start(f32[16,128]{1,0:T(8,128)S(1)} %get-tuple-element.168), channel_id=1, source_target_pairs={{0,1},{1,0},{2,3},{3,2},{4,5},{5,4},{6,7},{7,6},{8,9},{9,8},{10,11... | collective-permute-start | bytes 24584 | tf_op jit(solution)/shard_map/ppermute | solution.py:678
  139.4 2.5 %collective-permute-start.24 = (f32[16,128]{1,0:T(8,128)S(1)}, f32[16,128]{1,0:T(8,128)S(1)}, u32[]{:S(2)}, u32[]{:S(2)}) collective-permute-start(f32[16,128]{1,0:T(8,128)S(1)} %add.47), channel_id=1, source_target_pairs={{0,2},{1,3},{2,0},{3,1},{4,6},{5,7},{6,4},{7,5},{8,10},{9,11},{10,... | collective-permute-start | bytes 24584 | tf_op jit(solution)/shard_map/ppermute | solution.py:678
  141.9 3.7 %collective-permute-start.25 = (f32[16,128]{1,0:T(8,128)S(1)}, f32[16,128]{1,0:T(8,128)S(1)}, u32[]{:S(2)}, u32[]{:S(2)}) collective-permute-start(f32[16,128]{1,0:T(8,128)S(1)} %add.48), channel_id=1, source_target_pairs={{0,6},{1,7},{2,4},{3,5},{4,2},{5,3},{6,0},{7,1},{8,14},{9,15},{10,... | collective-permute-start | bytes 24584 | tf_op jit(solution)/shard_map/ppermute | solution.py:678
  145.6 25.0 %copy-start = (f32[10,8,128]{2,1,0:T(8,128)S(1)}, f32[10,8,128]{2,1,0:T(8,128)}, u32[]{:S(2)}) copy-start(f32[10,8,128]{2,1,0:T(8,128)} %head.1) | copy-start | bytes 122884
